TPU v7x, 512 devices: a whole 4x8x8 slice. The times are simulated.
512 devices in a mesh: grp: 16 (over x_lo, y), row: 32 (over x_hi, z, core).
Axes of the slice: x: 4 (x_hi: 2, x_lo: 2; x = x_hi * 2 + x_lo), y: 8, z: 8, core: 2. Of those that a mesh axis runs over, the one named last changes fastest.
Arguments:
- q_proj: bfloat16 [256, 131072], P(None, ('grp', 'row')), may hold values from -6 to 6
- k_proj: bfloat16 [256, 131072], P(None, ('grp', 'row')), may hold values from -6 to 6
- v_proj: bfloat16 [256, 131072], P(None, ('grp', 'row')), may hold values from -6 to 6
- filter_spectrum: float32 [2, 32, 256, 32, 256], P(None, 'grp', None, 'row'), may hold values from -6 to 6
- skip_gain: float32 [256], replicated, may hold values from -3 to 3
Outputs:
- gated: float32 [256, 131072], P(None, ('grp', 'row'))
All inputs are finite; a program needn't handle non-finite values.
Results may differ from a plain program's by a relative error of at most 0.0029.
Values may be sent and summed in bfloat16 or wider, within the bound.
No kernel may reach another device: no remote copies, remote signals or barrier semaphores. Data moves between devices by JAX's collectives and lax.ppermute only.
A program may use at most 64 MiB of HBM per device.

v0:
```python
import functools
import math

import jax
import jax.numpy as jnp
import ml_dtypes
import numpy as np
from jax import lax
from jax.experimental import pallas as pl
from jax.experimental.pallas import tpu as pltpu
from jax.sharding import PartitionSpec as P

both_axes = ("grp", "row")
LANES = 128
vmem_params = pltpu.CompilerParams(vmem_limit_bytes=40 * 1024 * 1024)


def split_bf16(table):
    table = np.asarray(table, np.float32)
    high = table.astype(ml_dtypes.bfloat16)
    low = (table - high.astype(np.float32)).astype(ml_dtypes.bfloat16)
    return high, low


def unit_angles(numer, denom):
    return 2.0 * math.pi / denom * (numer % denom).astype(np.float64)


@functools.lru_cache
def tables(groups, rows, length):
    blocks = groups * rows
    padded = 2 * blocks * length
    outer = np.arange(blocks, dtype=np.int64)
    inner = np.arange(length, dtype=np.int64)
    forward, backward, twist = [], [], []
    for parity in range(2):
        low = 2 * (outer // rows) + parity + 2 * groups * (outer % rows)
        theta = unit_angles(low[:, None] * outer[None, :], 2 * blocks)
        stacked = np.concatenate([np.cos(theta), -np.sin(theta)], axis=0)
        forward.append(np.stack(split_bf16(stacked)))
        backward.append(np.stack(split_bf16(stacked.T / padded)))
        phi = unit_angles(low[:, None] * inner[None, :], padded)
        twist.append(np.stack([np.cos(phi), np.sin(phi)]).astype(np.float32))
    angle = unit_angles(inner[:, None] * inner[None, :], length)
    cosine, sine = np.cos(angle), np.sin(angle)
    inner_forward = np.stack(split_bf16(np.block([[cosine, -sine], [sine, cosine]])))
    inner_backward = np.stack(split_bf16(np.block([[cosine, sine], [-sine, cosine]])))
    return np.stack(forward), np.stack(backward), np.stack(twist), inner_forward, inner_backward


def dot(left, right):
    return jnp.dot(left, right, preferred_element_type=jnp.float32)


def halves(value):
    high = value.astype(jnp.bfloat16)
    return high, (value - high.astype(jnp.float32)).astype(jnp.bfloat16)


def pack_kernel(k_ref, v_ref, filter_ref, out_ref, wide):
    channels = k_ref.shape[0]
    for part in range(2):
        for parity in range(2):
            first = (part * 2 + parity) * 2 * channels
            for half in range(2):
                wide[pl.ds(6 * parity + 2 * part + half, channels, stride=12), :] = filter_ref[
                    pl.ds(first + half, channels, stride=2), :
                ]
    product = k_ref[...].astype(jnp.float32) * v_ref[...].astype(jnp.float32)
    product = product.astype(jnp.bfloat16).astype(jnp.float32)
    for parity in range(2):
        for half in range(2):
            wide[pl.ds(6 * parity + 4 + half, channels, stride=12), :] = product[
                :, half * LANES : (half + 1) * LANES
            ]
    out_ref[...] = wide[...].astype(jnp.bfloat16)


def transform_kernel(
    got_ref, forward_ref, backward_ref, twist_ref, inner_f_ref, inner_b_ref, out_ref, wide, narrow
):
    blocks = got_ref.shape[0] // 6
    length = 2 * LANES
    wide[...] = got_ref[...].astype(jnp.float32)

    def piece(index):
        return jnp.concatenate(
            [wide[pl.ds(2 * index + half, blocks, stride=6), :] for half in range(2)], axis=1
        )

    signal = piece(2).astype(jnp.bfloat16)
    field = dot(forward_ref[0], signal) + dot(forward_ref[1], signal)
    real, imag = field[:blocks], field[blocks:]
    cosine, sine = twist_ref[0], twist_ref[1]
    high, low = halves(
        jnp.concatenate([real * cosine + imag * sine, imag * cosine - real * sine], axis=1)
    )
    spectrum = dot(high, inner_f_ref[0]) + (dot(low, inner_f_ref[0]) + dot(high, inner_f_ref[1]))
    real, imag = spectrum[:, :length], spectrum[:, length:]
    resp_real, resp_imag = piece(0), piece(1)
    high, low = halves(
        jnp.concatenate(
            [real * resp_real - imag * resp_imag, real * resp_imag + imag * resp_real], axis=1
        )
    )
    back = dot(high, inner_b_ref[0]) + (dot(low, inner_b_ref[0]) + dot(high, inner_b_ref[1]))
    real, imag = back[:, :length], back[:, length:]
    high, low = halves(
        jnp.concatenate([real * cosine - imag * sine, imag * cosine + real * sine], axis=0)
    )
    conv = dot(backward_ref[0], high) + (dot(backward_ref[1], high) + dot(backward_ref[0], low))
    for half in range(2):
        narrow[pl.ds(half, blocks, stride=2), :] = conv[:, half * LANES : (half + 1) * LANES]
    out_ref[...] = narrow[...].astype(jnp.bfloat16)


def gate_kernel(got_ref, q_ref, k_ref, v_ref, gain_ref, out_ref, wide):
    channels = q_ref.shape[0]
    wide[...] = got_ref[...].astype(jnp.float32)
    conv = jnp.concatenate(
        [
            wide[pl.ds(half, channels, stride=4), :] + wide[pl.ds(2 + half, channels, stride=4), :]
            for half in range(2)
        ],
        axis=1,
    )
    signal = (k_ref[...].astype(jnp.float32) * v_ref[...].astype(jnp.float32)).astype(jnp.bfloat16)
    out_ref[...] = q_ref[...].astype(jnp.float32) * (
        conv + gain_ref[...] * signal.astype(jnp.float32)
    )


def body(q_proj, k_proj, v_proj, filter_spectrum, skip_gain):
    channels, length = q_proj.shape
    groups, rows = lax.axis_size("grp"), lax.axis_size("row")
    blocks = groups * rows
    parity = lax.axis_index("row") % 2
    forward, backward, twist, inner_f, inner_b = tables(groups, rows, length)

    def mine(table):
        return lax.dynamic_index_in_dim(jnp.asarray(table), parity, 0, keepdims=False)

    with jax.named_scope("pack"):
        outgoing = pl.pallas_call(
            pack_kernel,
            out_shape=jax.ShapeDtypeStruct((6 * blocks, LANES), jnp.bfloat16),
            scratch_shapes=[pltpu.VMEM((6 * blocks, LANES), jnp.float32)],
            compiler_params=vmem_params,
        )(k_proj, v_proj, filter_spectrum.reshape(8 * channels, LANES))
    with jax.named_scope("scatter_channels"):
        incoming = lax.all_to_all(
            outgoing.reshape(blocks, 3, 2, LANES), both_axes, 0, 0, tiled=True
        )
    with jax.named_scope("transform"):
        partial_conv = pl.pallas_call(
            transform_kernel,
            out_shape=jax.ShapeDtypeStruct((2 * blocks, LANES), jnp.bfloat16),
            scratch_shapes=[
                pltpu.VMEM((6 * blocks, LANES), jnp.float32),
                pltpu.VMEM((2 * blocks, LANES), jnp.float32),
            ],
            compiler_params=vmem_params,
        )(
            incoming.reshape(6 * blocks, LANES),
            mine(forward),
            mine(backward),
            mine(twist),
            jnp.asarray(inner_f),
            jnp.asarray(inner_b),
        )
    with jax.named_scope("return_positions"):
        returned = lax.all_to_all(
            partial_conv.reshape(blocks, 2, LANES), both_axes, 0, 0, tiled=True
        )
    with jax.named_scope("gate"):
        return pl.pallas_call(
            gate_kernel,
            out_shape=jax.ShapeDtypeStruct((channels, length), jnp.float32),
            scratch_shapes=[pltpu.VMEM((2 * blocks, LANES), jnp.float32)],
            compiler_params=vmem_params,
        )(returned.reshape(2 * blocks, LANES), q_proj, k_proj, v_proj, skip_gain[:, None])


def solution(mesh):
    placed = (
        P(None, ("grp", "row")),
        P(None, ("grp", "row")),
        P(None, ("grp", "row")),
        P(None, "grp", None, "row", None),
        P(),
    )
    return jax.shard_map(
        body, mesh=mesh, in_specs=placed, out_specs=P(None, ("grp", "row")), check_vma=False
    )
```

profile of v0, /device:TPU:1, one launch (start us, length us, event | category | flops | bytes accessed | tf_op | source)
XLA Modules:
  0.0 94.0 jit_solution(17457608121517743630)
XLA Ops:
  0.0 1.2 %copy-done.1 = f32[2,2,256,1,256]{4,3,2,1,0:T(1,128)S(1)} copy-done((f32[2,2,256,1,256]{4,3,2,1,0:T(1,128)S(1)}, f32[2,2,256,1,256]{4,3,2,1,0:T(1,128)}, u32[]{:S(2)}) %copy-start.1) | copy-done | bytes 1048600
  1.2 0.9 copy-done.4
  2.1 0.9 copy-done.6
  3.0 1.2 %pack.1 = bf16[3072,128]{1,0:T(8,128)(2,1)} custom-call(bf16[256,256]{1,0:T(8,128)(2,1)S(1)} %copy-done.4, bf16[256,256]{1,0:T(8,128)(2,1)S(1)} %copy-done.6, f32[2048,128]{1,0:T(8,128)S(1)} %bitcast.12), custom_call_target="tpu_custom_call" | custom-call | tf_op jit(solution)/shard_map/pack/pallas_call | solution.py:144
  4.2 24.0 %all-to-all-start = ((bf16[512,3,2,128]{3,2,1,0:T(2,128)(2,1)}), bf16[512,3,2,128]{3,2,1,0:T(2,128)(2,1)}, u32[]{:S(2)}, u32[]{:S(2)}) async-start(bf16[512,3,2,128]{3,2,1,0:T(2,128)(2,1)} %bitcast.1), calls=%async_computation | async-start | bytes 1572864 | tf_op jit(solution)/shard_map/scatter_channels/all_to_all | solution.py:151
  28.2 0.0 copy-done.10
  28.2 0.1 dynamic-slice_bitcast_fusion.2.twist_ref
  28.3 0.0 copy-start.9
  28.3 1.9 %dynamic-slice_bitcast_fusion.1.forward_ref = bf16[2,1024,512]{2,1,0:T(8,128)(2,1)S(1)} fusion(bf16[2,2,1024,512]{3,2,1,0:T(8,128)(2,1)} %constant.39.clone, s32[]{:T(128)S(6)} %select_n.16), kind=kLoop, calls=%fused_computation.1 | loop fusion | bytes 4194308 | tf_op jit(solution)/shard_map/transform/jit(dynamic_index_in_dim)/squeeze | solution.py:141
  30.2 0.9 copy-done.9
  31.1 1.5 %dynamic-slice_bitcast_fusion.backward_ref = bf16[2,512,1024]{2,1,0:T(8,128)(2,1)} fusion(bf16[2,2,512,1024]{3,2,1,0:T(8,128)(2,1)S(1)} %copy-done.9, s32[]{:T(128)S(6)} %select_n.16), kind=kLoop, calls=%fused_computation | loop fusion | bytes 4194308 | tf_op jit(solution)/shard_map/transform/jit(dynamic_index_in_dim)/squeeze | solution.py:141
  32.6 21.7 %all-to-all-done = bf16[512,3,2,128]{3,2,1,0:T(2,128)(2,1)} async-done(((bf16[512,3,2,128]{3,2,1,0:T(2,128)(2,1)}), bf16[512,3,2,128]{3,2,1,0:T(2,128)(2,1)}, u32[]{:S(2)}, u32[]{:S(2)}) %all-to-all-start) | async-done | bytes 786464 | tf_op jit(solution)/shard_map/scatter_channels/all_to_all | solution.py:151
  54.4 1.6 %copy-done = bf16[2,512,1024]{2,1,0:T(8,128)(2,1)S(1)} copy-done((bf16[2,512,1024]{2,1,0:T(8,128)(2,1)S(1)}, bf16[2,512,1024]{2,1,0:T(8,128)(2,1)}, u32[]{:S(2)}) %copy-start) | copy-done | bytes 2097176
  56.0 1.2 %copy-done.2 = bf16[2,512,512]{2,1,0:T(8,128)(2,1)S(1)} copy-done((bf16[2,512,512]{2,1,0:T(8,128)(2,1)S(1)}, bf16[2,512,512]{2,1,0:T(8,128)(2,1)}, u32[]{:S(2)}) %copy-start.2) | copy-done | bytes 1048600
  57.2 1.2 %copy-done.3 = bf16[2,512,512]{2,1,0:T(8,128)(2,1)S(1)} copy-done((bf16[2,512,512]{2,1,0:T(8,128)(2,1)S(1)}, bf16[2,512,512]{2,1,0:T(8,128)(2,1)}, u32[]{:S(2)}) %copy-start.3) | copy-done | bytes 1048600
  58.4 8.1 %transform.1 = bf16[1024,128]{1,0:T(8,128)(2,1)} custom-call(bf16[3072,128]{1,0:T(8,128)(2,1)} %bitcast.2.got_ref, bf16[2,1024,512]{2,1,0:T(8,128)(2,1)S(1)} %dynamic-slice_bitcast_fusion.1.forward_ref, bf16[2,512,1024]{2,1,0:T(8,128)(2,1)S(1)} %copy-done, f32[2,512,256]{2,1,0:T(8,128)S(1)} %dynamic-slice_bitcast_fusion.2.twist_ref, ...), custom_call_target="tpu_custom_call" | custom-call | tf_op jit(solution)/shard_map/transform/pallas_call | solution.py:155
  66.5 9.5 %all-to-all-start.1 = ((bf16[512,2,128]{2,1,0:T(2,128)(2,1)}), bf16[512,2,128]{2,1,0:T(2,128)(2,1)S(1)}, u32[]{:S(2)}, u32[]{:S(2)}) async-start(bf16[512,2,128]{2,1,0:T(2,128)(2,1)} %bitcast.6), calls=%async_computation.1 | async-start | bytes 524288 | tf_op jit(solution)/shard_map/return_positions/all_to_all | solution.py:172
  76.0 0.0 copy-done.11
  76.0 0.1 copy.11.gain_ref
  76.2 17.0 %all-to-all-done.1 = bf16[512,2,128]{2,1,0:T(2,128)(2,1)S(1)} async-done(((bf16[512,2,128]{2,1,0:T(2,128)(2,1)}), bf16[512,2,128]{2,1,0:T(2,128)(2,1)S(1)}, u32[]{:S(2)}, u32[]{:S(2)}) %all-to-all-start.1) | async-done | bytes 262176 | tf_op jit(solution)/shard_map/return_positions/all_to_all | solution.py:172
  93.2 0.0 copy-done.5
  93.2 0.0 copy-done.7
  93.2 0.0 copy-done.8
  93.2 0.9 gate.1
  (11 shorter events, 0.0 us)
Async XLA Ops:
  0.0 1.2 %copy-start.1 = (f32[2,2,256,1,256]{4,3,2,1,0:T(1,128)S(1)}, f32[2,2,256,1,256]{4,3,2,1,0:T(1,128)}, u32[]{:S(2)}) copy-start(f32[2,2,256,1,256]{4,3,2,1,0:T(1,128)} %param.13) | copy-start | bytes 3145732
  1.2 0.9 copy-start.4
  2.1 0.9 copy-start.6
  3.0 25.2 %copy-start.10 = (f32[2,2,512,256]{3,2,1,0:T(8,128)S(1)}, f32[2,2,512,256]{3,2,1,0:T(8,128)}, u32[]{:S(2)}) copy-start(f32[2,2,512,256]{3,2,1,0:T(8,128)} %constant.41.clone) | copy-start | bytes 6291460
  4.2 50.1 %all-to-all-start = ((bf16[512,3,2,128]{3,2,1,0:T(2,128)(2,1)}), bf16[512,3,2,128]{3,2,1,0:T(2,128)(2,1)}, u32[]{:S(2)}, u32[]{:S(2)}) async-start(bf16[512,3,2,128]{3,2,1,0:T(2,128)(2,1)} %bitcast.1), calls=%async_computation | async-start | bytes 1572864 | tf_op jit(solution)/shard_map/scatter_channels/all_to_all | solution.py:151
  28.3 2.8 %copy-start.9 = (bf16[2,2,512,1024]{3,2,1,0:T(8,128)(2,1)S(1)}, bf16[2,2,512,1024]{3,2,1,0:T(8,128)(2,1)}, u32[]{:S(2)}) copy-start(bf16[2,2,512,1024]{3,2,1,0:T(8,128)(2,1)} %constant.40.clone) | copy-start | bytes 12582916
  54.4 1.6 %copy-start = (bf16[2,512,1024]{2,1,0:T(8,128)(2,1)S(1)}, bf16[2,512,1024]{2,1,0:T(8,128)(2,1)}, u32[]{:S(2)}) copy-start(bf16[2,512,1024]{2,1,0:T(8,128)(2,1)} %dynamic-slice_bitcast_fusion.backward_ref) | copy-start | bytes 6291460
  56.0 1.2 %copy-start.2 = (bf16[2,512,512]{2,1,0:T(8,128)(2,1)S(1)}, bf16[2,512,512]{2,1,0:T(8,128)(2,1)}, u32[]{:S(2)}) copy-start(bf16[2,512,512]{2,1,0:T(8,128)(2,1)} %constant.42.clone.inner_f_ref) | copy-start | bytes 3145732
  57.2 1.2 %copy-start.3 = (bf16[2,512,512]{2,1,0:T(8,128)(2,1)S(1)}, bf16[2,512,512]{2,1,0:T(8,128)(2,1)}, u32[]{:S(2)}) copy-start(bf16[2,512,512]{2,1,0:T(8,128)(2,1)} %constant.43.clone.inner_b_ref) | copy-start | bytes 3145732
  58.4 17.6 %copy-start.11 = (f32[256]{0:T(256)S(1)}, f32[256]{0:T(256)}, u32[]{:S(2)}) copy-start(f32[256]{0:T(256)} %param.14) | copy-start | bytes 3076
  58.4 34.8 %copy-start.5 = (bf16[256,256]{1,0:T(8,128)(2,1)S(1)}, bf16[256,256]{1,0:T(8,128)(2,1)}, u32[]{:S(2)}) copy-start(bf16[256,256]{1,0:T(8,128)(2,1)} %k_ref.3) | copy-start | bytes 393220
  58.4 34.8 %copy-start.7 = (bf16[256,256]{1,0:T(8,128)(2,1)S(1)}, bf16[256,256]{1,0:T(8,128)(2,1)}, u32[]{:S(2)}) copy-start(bf16[256,256]{1,0:T(8,128)(2,1)} %v_ref.3) | copy-start | bytes 393220
  58.4 34.8 %copy-start.8 = (bf16[256,256]{1,0:T(8,128)(2,1)S(1)}, bf16[256,256]{1,0:T(8,128)(2,1)}, u32[]{:S(2)}) copy-start(bf16[256,256]{1,0:T(8,128)(2,1)} %q_ref.1) | copy-start | bytes 393220
  66.5 26.7 %all-to-all-start.1 = ((bf16[512,2,128]{2,1,0:T(2,128)(2,1)}), bf16[512,2,128]{2,1,0:T(2,128)(2,1)S(1)}, u32[]{:S(2)}, u32[]{:S(2)}) async-start(bf16[512,2,128]{2,1,0:T(2,128)(2,1)} %bitcast.6), calls=%async_computation.1 | async-start | bytes 524288 | tf_op jit(solution)/shard_map/return_positions/all_to_all | solution.py:172
where the time goes:
time: 94.4 us; the launch traced here: 94 us
  waiting for transfers between devices  38.7 us (41%)
  starting transfers between devices  33.5 us (35%)
  local copies, waits for them, and re-layouts  11.6 us (12%)
  Pallas kernels  10.1 us (11%)
    all_to_all x1, starting transfers between devices, body(): lax.all_to_all(outgoing.reshape(blocks, 3, 2, LANES), both_axes, 0, 0, ti...  24 us
    all_to_all x1, waiting for transfers between devices, body(): lax.all_to_all(outgoing.reshape(blocks, 3, 2, LANES), both_axes, 0, 0, ti...  21.7 us
    all_to_all x1, waiting for transfers between devices, body(): lax.all_to_all(partial_conv.reshape(blocks, 2, LANES), both_axes, 0, 0, t...  17 us
    all_to_all x1, starting transfers between devices, body(): lax.all_to_all(partial_conv.reshape(blocks, 2, LANES), both_axes, 0, 0, t...  9.54 us
    pallas_call x1, Pallas kernels, body(): pl.pallas_call(transform_kernel, out_shape=jax.ShapeDtypeStruct((2 * bloc...  8.05 us
    unnamed x24, local copies, waits for them, and re-layouts  8.01 us
    squeeze x3, local copies, waits for them, and re-layouts, mine(): lax.dynamic_index_in_dim(jnp.asarray(table), parity, 0, keepdims=False)  3.46 us
  transfers between devices with their start and end apart: 2, of which 2 were waited for; matrix products, arithmetic and copies ran while one was open for 4% of the time, Pallas kernels for 0%

commit v1 on v0

v1 whole, which is shorter than its diff:
```python
import functools
import math

import jax
import jax.numpy as jnp
import ml_dtypes
import numpy as np
from jax import lax
from jax.experimental import pallas as pl
from jax.experimental.pallas import tpu as pltpu
from jax.sharding import PartitionSpec as P

both_axes = ("grp", "row")
LANES = 128
CHUNKS = 4


def split_bf16(table):
    table = np.asarray(table, np.float32)
    high = table.astype(ml_dtypes.bfloat16)
    low = (table - high.astype(np.float32)).astype(ml_dtypes.bfloat16)
    return high, low


def unit_angles(numer, denom):
    return 2.0 * math.pi / denom * (numer % denom).astype(np.float64)


@functools.lru_cache
def tables(groups, rows, length):
    blocks, padded = groups * rows, 2 * groups * rows * length
    pair = np.arange(blocks // 2, dtype=np.int64)
    group, half_row = pair // (rows // 2), pair % (rows // 2)
    inner = np.arange(length, dtype=np.int64)
    forward, backward, fine, coarse = [], [], [], []
    for core in range(2):
        low_parts = (2 * np.arange(groups)[None, :] + np.arange(2)[:, None]).reshape(-1)
        high_parts = 2 * groups * (2 * np.arange(rows // 2) + core)
        low = (low_parts[:, None] + high_parts[None, :]).reshape(-1)
        outer = group * rows + 2 * half_row + core
        theta = unit_angles(low[:, None] * outer[None, :], 2 * blocks)
        matrix = np.concatenate([np.cos(theta), -np.sin(theta)], axis=0)
        forward.append(np.stack(split_bf16(matrix)))
        backward.append(np.stack(split_bf16(matrix.T / padded)))
        steps = np.concatenate([inner, np.full(LANES, (1 - 2 * core) * length)])
        for parts, store in ((low_parts, fine), (high_parts, coarse)):
            phi = unit_angles(parts[:, None] * steps[None, :], padded)
            store.append(np.stack([np.cos(phi), np.sin(phi)]).astype(np.float32))
    angle = unit_angles(inner[:, None] * inner[None, :], length)
    cosine, sine = np.cos(angle), np.sin(angle)
    mixed = np.stack(split_bf16(np.block([[cosine, -sine], [sine, cosine]])))
    stacked = [np.stack(t) for t in (forward, fine, coarse)]
    return [*stacked, mixed], np.stack(backward)


def dot(left, right):
    return jnp.dot(left, right, preferred_element_type=jnp.float32)


def halves(value):
    high = value.astype(jnp.bfloat16)
    return high, (value - high.astype(jnp.float32)).astype(jnp.bfloat16)


def dot_wide(high, low, table):
    return dot(
        jnp.concatenate([high, low, high], axis=1),
        jnp.concatenate([table[0], table[0], table[1]], axis=0),
    )


def rotate(real, imag, cosine, sine):
    return real * cosine + imag * sine, imag * cosine - real * sine


def joined(ref, first, step, count):
    return jnp.concatenate(
        [ref[pl.ds(first + half, count, stride=step), :] for half in range(2)], axis=1
    )


def pack_kernel(k_hbm, v_hbm, filter_hbm, out_hbm, k_ref, v_ref, filter_ref, wide, out_ref, sems):
    channels = k_ref.shape[0]
    chunk = channels // CHUNKS
    fetch = [pltpu.make_async_copy(k_hbm, k_ref, sems.at[0]),
             pltpu.make_async_copy(v_hbm, v_ref, sems.at[1])]
    for index in range(CHUNKS):
        rows = pl.ds(2 * index * chunk, 2 * chunk)
        fetch.append(
            pltpu.make_async_copy(
                filter_hbm.at[:, rows], filter_ref.at[:, rows], sems.at[2 + index]
            )
        )
    for copy in fetch:
        copy.start()
    fetch[0].wait()
    fetch[1].wait()
    product = k_ref[...].astype(jnp.float32) * v_ref[...].astype(jnp.float32)
    product = product.astype(jnp.bfloat16).astype(jnp.float32)
    for half in range(2):
        wide[pl.ds(8 + half, channels, stride=10), :] = product[
            :, half * LANES : (half + 1) * LANES
        ]
    send = []
    for index in range(CHUNKS):
        fetch[2 + index].wait()
        first = 10 * index * chunk
        for part in range(2):
            for low in range(2):
                for half in range(2):
                    wide[pl.ds(first + 4 * low + 2 * part + half, chunk, stride=10), :] = (
                        filter_ref[
                            2 * part + low, pl.ds(2 * index * chunk + half, chunk, stride=2), :
                        ]
                    )
        rows = pl.ds(first, 10 * chunk)
        out_ref[rows, :] = wide[rows, :].astype(jnp.bfloat16)
        send.append(
            pltpu.make_async_copy(out_ref.at[rows], out_hbm.at[rows], sems.at[2 + CHUNKS + index])
        )
        send[index].start()
    for copy in send:
        copy.wait()


def tables_kernel(*refs):
    core = lax.axis_index("row") % 2
    count = (len(refs) - 1) // 2
    sems = refs[-1]
    copies = []
    for index in range(count):
        source = refs[index] if index == count - 1 else refs[index].at[core]
        copies.append(pltpu.make_async_copy(source, refs[count + index], sems.at[index]))
        copies[index].start()
    for copy in copies:
        copy.wait()


def own_kernel(got_ref, forward_ref, fine_ref, coarse_ref, field_ref, response_ref, twist_ref, wide):
    pairs = got_ref.shape[0] // 10
    wide[...] = got_ref[...].astype(jnp.float32)
    signal = joined(wide, 8, 10, pairs).astype(jnp.bfloat16)
    field_ref[...] = dot(forward_ref[0], signal) + dot(forward_ref[1], signal)
    for part in range(2):
        for low in range(2):
            response_ref[part, low * pairs : (low + 1) * pairs, :] = joined(
                wide, 4 * low + 2 * part, 10, pairs
            )
    count = coarse_ref.shape[1]
    cosine, sine = coarse_ref[0], coarse_ref[1]
    for index in range(fine_ref.shape[1]):
        rows = slice(index * count, (index + 1) * count)
        fine_cos, fine_sin = fine_ref[0, index : index + 1], fine_ref[1, index : index + 1]
        twist_ref[0, rows, :] = cosine * fine_cos - sine * fine_sin
        twist_ref[1, rows, :] = sine * fine_cos + cosine * fine_sin


def spectrum_kernel(
    backward_hbm, other_ref, forward_ref, field_ref, response_ref, twist_ref, mixed_ref,
    sent_ref, kept_ref, wide, backward_ref, sem,
):
    core = lax.axis_index("row") % 2
    fetch = pltpu.make_async_copy(backward_hbm.at[core], backward_ref, sem)
    fetch.start()
    pairs = other_ref.shape[0] // 2
    count, length = 2 * pairs, 2 * LANES
    wide[...] = other_ref[...].astype(jnp.float32)
    signal = joined(wide, 0, 2, pairs).astype(jnp.bfloat16)
    field = dot(forward_ref[0], signal) + dot(forward_ref[1], signal)
    shift_cos = jnp.concatenate([twist_ref[0, :, length:]] * 2, axis=1)
    shift_sin = jnp.concatenate([twist_ref[1, :, length:]] * 2, axis=1)
    cosine, sine = twist_ref[0, :, :length], twist_ref[1, :, :length]
    real, imag = rotate(field[:count], field[count:], shift_cos, shift_sin)
    real, imag = rotate(field_ref[:count] + real, field_ref[count:] + imag, cosine, sine)
    high, low = halves(jnp.concatenate([real, imag], axis=1))
    spectrum = dot_wide(high, low, mixed_ref)
    real, imag = spectrum[:, :length], spectrum[:, length:]
    resp_real, resp_imag = response_ref[0], response_ref[1]
    high, low = halves(
        jnp.concatenate(
            [real * resp_imag + imag * resp_real, real * resp_real - imag * resp_imag], axis=1
        )
    )
    back = dot_wide(high, low, mixed_ref)
    real, imag = rotate(back[:, length:], back[:, :length], cosine, -sine)
    fetch.wait()

    def positions(real, imag):
        high, low = halves(jnp.concatenate([real, imag], axis=0))
        return dot(
            jnp.concatenate([backward_ref[0], backward_ref[0], backward_ref[1]], axis=1),
            jnp.concatenate([high, low, high], axis=0),
        )

    sent_ref[...] = positions(*rotate(real, imag, shift_cos, -shift_sin))
    kept_ref[...] = positions(real, imag)


def add_kernel(kept_ref, came_ref, out_ref, wide):
    pairs = kept_ref.shape[0]
    conv = kept_ref[...] + came_ref[...]
    for half in range(2):
        wide[pl.ds(half, pairs, stride=2), :] = conv[:, half * LANES : (half + 1) * LANES]
    out_ref[...] = wide[...].astype(jnp.bfloat16)


def gate_kernel(got_ref, q_ref, k_ref, v_ref, gain_ref, out_ref, wide):
    channels = q_ref.shape[0]
    wide[...] = got_ref[...].astype(jnp.float32)
    conv = joined(wide, 0, 2, channels)
    signal = (k_ref[...].astype(jnp.float32) * v_ref[...].astype(jnp.float32)).astype(jnp.bfloat16)
    out_ref[...] = q_ref[...].astype(jnp.float32) * (
        conv + gain_ref[...] * signal.astype(jnp.float32)
    )


def call(kernel, shapes, scratch, megabytes, anywhere=0, out_anywhere=False, operands=0):
    extra = {}
    if anywhere:
        extra["in_specs"] = [pl.BlockSpec(memory_space=pl.ANY)] * anywhere
        extra["in_specs"] += [pl.BlockSpec(memory_space=pltpu.VMEM)] * (operands - anywhere)
    if out_anywhere:
        extra["out_specs"] = pl.BlockSpec(memory_space=pl.ANY)
    return pl.pallas_call(
        kernel,
        out_shape=shapes,
        scratch_shapes=scratch,
        compiler_params=pltpu.CompilerParams(vmem_limit_bytes=megabytes * 1024 * 1024),
        **extra,
    )


def body(q_proj, k_proj, v_proj, filter_spectrum, skip_gain):
    channels, length = q_proj.shape
    groups, rows = lax.axis_size("grp"), lax.axis_size("row")
    pairs = groups * rows // 2
    same_core = [list(range(c, groups * rows, 2)) for c in range(2)]
    swap = [(i, i ^ 1) for i in range(rows)]
    f32, bf16 = jnp.float32, jnp.bfloat16
    shape = jax.ShapeDtypeStruct

    def exchange(tensor, pieces):
        return lax.all_to_all(
            tensor.reshape(pairs, pieces, 2, LANES), both_axes, 0, 0,
            tiled=True, axis_index_groups=same_core,
        )

    with jax.named_scope("pack"):
        outgoing = call(
            pack_kernel, shape((10 * channels, LANES), bf16),
            [pltpu.VMEM((channels, length), bf16)] * 2
            + [pltpu.VMEM((4, 2 * channels, LANES), f32), pltpu.VMEM((10 * channels, LANES), f32),
               pltpu.VMEM((10 * channels, LANES), bf16), pltpu.SemaphoreType.DMA((2 + 2 * CHUNKS,))],
            58, 3, True,
        )(k_proj, v_proj, filter_spectrum.reshape(4, 2 * channels, LANES))
    constants, backward = tables(groups, rows, length)
    constants = [jnp.asarray(table) for table in constants]
    outgoing, constants = lax.optimization_barrier((outgoing, constants))
    with jax.named_scope("to_channels"):
        incoming = exchange(outgoing, 5)
    with jax.named_scope("tables"):
        local = [shape(t.shape[1:], t.dtype) for t in constants[:-1]]
        local.append(shape(constants[-1].shape, constants[-1].dtype))
        parts = call(
            tables_kernel, local, [pltpu.SemaphoreType.DMA((len(local),))], 12, len(local)
        )(*constants)
    incoming, parts = lax.optimization_barrier((incoming, parts))
    forward, fine, coarse, mixed = parts
    with jax.named_scope("signal_swap"):
        other = lax.ppermute(incoming[:, 4].reshape(2 * pairs, LANES), "row", swap)
    with jax.named_scope("own_positions"):
        field, response, twist = call(
            own_kernel,
            [shape((4 * pairs, length), f32), shape((2, 2 * pairs, length), f32),
             shape((2, 2 * pairs, length + LANES), f32)],
            [pltpu.VMEM((10 * pairs, LANES), f32)], 8,
        )(incoming.reshape(10 * pairs, LANES), forward, fine, coarse)
    with jax.named_scope("spectrum"):
        sent, kept = call(
            spectrum_kernel, [shape((pairs, length), f32)] * 2,
            [pltpu.VMEM((2 * pairs, LANES), f32), pltpu.VMEM(backward.shape[1:], bf16),
             pltpu.SemaphoreType.DMA], 20, 1, operands=7,
        )(jnp.asarray(backward), other, forward, field, response, twist, mixed)
    with jax.named_scope("result_swap"):
        came = lax.ppermute(sent, "row", swap)
    with jax.named_scope("add_cores"):
        result = call(
            add_kernel, shape((2 * pairs, LANES), bf16), [pltpu.VMEM((2 * pairs, LANES), f32)], 4
        )(kept, came)
    with jax.named_scope("to_positions"):
        returned = exchange(result, 1)
    with jax.named_scope("gate"):
        return call(
            gate_kernel, shape((channels, length), f32),
            [pltpu.VMEM((2 * channels, LANES), f32)], 4,
        )(returned.reshape(2 * channels, LANES), q_proj, k_proj, v_proj, skip_gain[:, None])


def solution(mesh):
    placed = (
        P(None, ("grp", "row")),
        P(None, ("grp", "row")),
        P(None, ("grp", "row")),
        P(None, "grp", None, "row", None),
        P(),
    )
    return jax.shard_map(
        body, mesh=mesh, in_specs=placed, out_specs=P(None, ("grp", "row")), check_vma=False
    )
```

time: 94.4 us -> 82.8 us (0.88)
  local copies, waits for them, and re-layouts: 11.6 us -> 3.06 us
  waiting for transfers between devices: 38.7 us -> 30.3 us
  starting transfers between devices: 33.5 us -> 40.4 us
  Pallas kernels: 10.1 us -> 8.17 us
    all_to_all x2, waiting for transfers between devices: 38.7 us -> 28.9 us  [exchange(): lax.all_to_all(tensor.reshape(pairs, pieces, 2, LANES), both_axes, 0, 0,...]
    ppermute x0 -> x2, starting transfers between devices: none -> 8.04 us  [the longest x1 5.77 us: body(): other = lax.ppermute(incoming[:, 4].reshape(2 * pairs, LANES), 'row', swap)]
    unnamed x24 -> x18, local copies, waits for them, and re-layouts: 8.01 us -> 2.84 us
    squeeze x3 -> x0, local copies, waits for them, and re-layouts: 3.46 us -> none  [mine(): lax.dynamic_index_in_dim(jnp.asarray(table), parity, 0, keepdims=False)]
    pallas_call x3 -> x6, Pallas kernels: 10.1 us -> 8.17 us  [the longest x1 3.43 us: body(): call(spectrum_kernel, [shape((pairs, length), f32)] * 2, [pltpu.VMEM((2 *...]
    ppermute x0 -> x2, waiting for transfers between devices: none -> 1.4 us  [the longest x1 1.15 us: body(): came = lax.ppermute(sent, 'row', swap)]
    all_to_all x2, starting transfers between devices: 33.5 us -> 32.4 us  [exchange(): lax.all_to_all(tensor.reshape(pairs, pieces, 2, LANES), both_axes, 0, 0,...]
  transfers between devices with their start and end apart: 2 -> 4, of which waited for: 2 -> 4; matrix products, arithmetic and copies ran while one was open for 4% -> 0% of each run, Pallas kernels for 0% -> 1%
where the time goes in v1:
time: 82.8 us; the launch traced here: 82.1 us
  starting transfers between devices  40.4 us (49%)
  waiting for transfers between devices  30.3 us (37%)
  Pallas kernels  8.17 us (10%)
  local copies, waits for them, and re-layouts  3.06 us (4%)
    all_to_all x2, starting transfers between devices, exchange(): lax.all_to_all(tensor.reshape(pairs, pieces, 2, LANES), both_axes, 0, 0,...  32.4 us
    all_to_all x2, waiting for transfers between devices, exchange(): lax.all_to_all(tensor.reshape(pairs, pieces, 2, LANES), both_axes, 0, 0,...  28.9 us
    ppermute x1, starting transfers between devices, body(): other = lax.ppermute(incoming[:, 4].reshape(2 * pairs, LANES), 'row', swap)  5.77 us
    pallas_call x1, Pallas kernels, body(): call(spectrum_kernel, [shape((pairs, length), f32)] * 2, [pltpu.VMEM((2 *...  3.43 us
    unnamed x18, local copies, waits for them, and re-layouts  2.84 us
    ppermute x1, starting transfers between devices, body(): came = lax.ppermute(sent, 'row', swap)  2.27 us
    pallas_call x1, Pallas kernels, body(): call(pack_kernel, shape((10 * channels, LANES), bf16), [pltpu.VMEM((chann...  2.15 us
  transfers between devices with their start and end apart: 4, of which 4 were waited for; matrix products, arithmetic and copies ran while one was open for 0% of the time, Pallas kernels for 1%

profile of v1, /device:TPU:1, one launch (start us, length us, event | category | flops | bytes accessed | tf_op | source)
XLA Modules:
  0.0 82.1 jit_solution(6886587775166415419)
XLA Ops:
  0.0 2.1 %pack.1 = bf16[2560,128]{1,0:T(8,128)(2,1)} custom-call(bf16[256,256]{1,0:T(8,128)(2,1)} %k_ref.1, bf16[256,256]{1,0:T(8,128)(2,1)} %v_ref.1, f32[4,512,128]{2,1,0:T(8,128)} %bitcast.12), custom_call_target="tpu_custom_call" | custom-call | tf_op jit(solution)/shard_map/pack/pallas_call | solution.py:249
  2.2 23.2 %all-to-all-start = ((bf16[256,5,2,128]{3,2,1,0:T(2,128)(2,1)}), bf16[256,5,2,128]{3,2,1,0:T(2,128)(2,1)S(1)}, u32[]{:S(2)}, u32[]{:S(2)}) async-start(bf16[256,5,2,128]{3,2,1,0:T(2,128)(2,1)} %bitcast.11), calls=%async_computation | async-start | bytes 1310720 | tf_op jit(solution)/shard_map/to_channels/all_to_all | solution.py:243
  25.4 0.0 copy-done.5
  25.4 0.0 copy-done.7
  25.4 0.0 copy-start
  25.4 1.6 %copy-done = bf16[2,2,1024,256]{3,2,1,0:T(8,128)(2,1)S(1)} copy-done((bf16[2,2,1024,256]{3,2,1,0:T(8,128)(2,1)S(1)}, bf16[2,2,1024,256]{3,2,1,0:T(8,128)(2,1)}, u32[]{:S(2)}) %copy-start) | copy-done | bytes 2097176
  27.0 1.2 %copy-done.2 = bf16[2,512,512]{2,1,0:T(8,128)(2,1)S(1)} copy-done((bf16[2,512,512]{2,1,0:T(8,128)(2,1)S(1)}, bf16[2,512,512]{2,1,0:T(8,128)(2,1)}, u32[]{:S(2)}) %copy-start.2) | copy-done | bytes 1048600
  28.2 0.4 tables.1
  28.6 17.0 %all-to-all-done = bf16[256,5,2,128]{3,2,1,0:T(2,128)(2,1)S(1)} async-done(((bf16[256,5,2,128]{3,2,1,0:T(2,128)(2,1)}), bf16[256,5,2,128]{3,2,1,0:T(2,128)(2,1)S(1)}, u32[]{:S(2)}, u32[]{:S(2)}) %all-to-all-start) | async-done | bytes 655392 | tf_op jit(solution)/shard_map/to_channels/all_to_all | solution.py:243
  45.6 0.1 slice.3
  45.7 5.8 %collective-permute-start = (bf16[512,128]{1,0:T(8,128)(2,1)S(1)}, bf16[512,128]{1,0:T(8,128)(2,1)S(1)}, u32[]{:S(2)}, u32[]{:S(2)}) collective-permute-start(bf16[512,128]{1,0:T(8,128)(2,1)S(1)} %bitcast.13), channel_id=1, source_target_pairs={{0,1},{1,0},{2,3},{3,2},{4,5},{5,4},{6,7},{7,6},{8,9},{9,8},{10,11... | collective-permute-start | bytes 393224 | tf_op jit(solution)/shard_map/signal_swap/ppermute | solution.py:270
  51.5 0.7 own_positions.1
  52.2 0.3 collective-permute-done.other_ref
  52.5 0.0 copy-done.1
  52.5 0.0 copy-start.6
  52.5 3.4 %spectrum.1 = (f32[256,256]{1,0:T(8,128)S(1)}, f32[256,256]{1,0:T(8,128)S(1)}) custom-call(bf16[2,2,256,1024]{3,2,1,0:T(8,128)(2,1)S(1)} %copy-done.1, bf16[512,128]{1,0:T(8,128)(2,1)S(1)} %collective-permute-done.other_ref, bf16[2,1024,256]{2,1,0:T(8,128)(2,1)S(1)} %get-tuple-element.34.forward_ref, f32[1024,256]{1,0:T(8,128)S(1)} %get-tuple-element.37.field_ref, ...), custom_call_target="tpu_custom_call" | custom-call | tf_op jit(solution)/shard_map/spectrum/pallas_call | solution.py:279
  55.9 2.3 %collective-permute-start.1 = (f32[256,256]{1,0:T(8,128)S(1)}, f32[256,256]{1,0:T(8,128)S(1)}, u32[]{:S(2)}, u32[]{:S(2)}) collective-permute-start(f32[256,256]{1,0:T(8,128)S(1)} %get-tuple-element.42), channel_id=1, source_target_pairs={{0,1},{1,0},{2,3},{3,2},{4,5},{5,4},{6,7},{7,6},{8,9},{9,8},{10,11... | collective-permute-start | bytes 786440 | tf_op jit(solution)/shard_map/result_swap/ppermute | solution.py:285
  58.2 1.2 %collective-permute-done.1.came_ref = f32[256,256]{1,0:T(8,128)S(1)} collective-permute-done((f32[256,256]{1,0:T(8,128)S(1)}, f32[256,256]{1,0:T(8,128)S(1)}, u32[]{:S(2)}, u32[]{:S(2)}) %collective-permute-start.1) | collective-permute-done | bytes 262176 | tf_op jit(solution)/shard_map/result_swap/ppermute | solution.py:285
  59.4 0.7 add_cores.1
  60.1 9.1 %all-to-all-start.1 = ((bf16[256,1,2,128]{3,2,1,0:T(2,128)(2,1)}), bf16[256,1,2,128]{3,2,1,0:T(2,128)(2,1)S(1)}, u32[]{:S(2)}, u32[]{:S(2)}) async-start(bf16[256,1,2,128]{3,2,1,0:T(2,128)(2,1)} %bitcast.5), calls=%async_computation.1 | async-start | bytes 262144 | tf_op jit(solution)/shard_map/to_positions/all_to_all | solution.py:243
  69.2 0.1 copy.17.gain_ref
  69.4 11.9 %all-to-all-done.1 = bf16[256,1,2,128]{3,2,1,0:T(2,128)(2,1)S(1)} async-done(((bf16[256,1,2,128]{3,2,1,0:T(2,128)(2,1)}), bf16[256,1,2,128]{3,2,1,0:T(2,128)(2,1)S(1)}, u32[]{:S(2)}, u32[]{:S(2)}) %all-to-all-start.1) | async-done | bytes 131104 | tf_op jit(solution)/shard_map/to_positions/all_to_all | solution.py:243
  81.3 0.0 copy-done.4
  81.3 0.8 gate.1
  (10 shorter events, 0.0 us)
Async XLA Ops:
  0.0 25.4 %copy-start.5 = (f32[2,2,32,384]{3,2,1,0:T(8,128)S(1)}, f32[2,2,32,384]{3,2,1,0:T(8,128)}, u32[]{:S(2)}) copy-start(f32[2,2,32,384]{3,2,1,0:T(8,128)} %constant.11.clone.refs_1_) | copy-start | bytes 589828
  0.0 25.4 %copy-start.7 = (f32[2,2,16,384]{3,2,1,0:T(8,128)S(1)}, f32[2,2,16,384]{3,2,1,0:T(8,128)}, u32[]{:S(2)}) copy-start(f32[2,2,16,384]{3,2,1,0:T(8,128)} %constant.12.clone.refs_2_) | copy-start | bytes 294916
  2.2 43.5 %all-to-all-start = ((bf16[256,5,2,128]{3,2,1,0:T(2,128)(2,1)}), bf16[256,5,2,128]{3,2,1,0:T(2,128)(2,1)S(1)}, u32[]{:S(2)}, u32[]{:S(2)}) async-start(bf16[256,5,2,128]{3,2,1,0:T(2,128)(2,1)} %bitcast.11), calls=%async_computation | async-start | bytes 1310720 | tf_op jit(solution)/shard_map/to_channels/all_to_all | solution.py:243
  25.4 1.6 %copy-start = (bf16[2,2,1024,256]{3,2,1,0:T(8,128)(2,1)S(1)}, bf16[2,2,1024,256]{3,2,1,0:T(8,128)(2,1)}, u32[]{:S(2)}) copy-start(bf16[2,2,1024,256]{3,2,1,0:T(8,128)(2,1)} %constant.10.clone.refs_0_) | copy-start | bytes 6291460
  27.0 1.2 %copy-start.2 = (bf16[2,512,512]{2,1,0:T(8,128)(2,1)S(1)}, bf16[2,512,512]{2,1,0:T(8,128)(2,1)}, u32[]{:S(2)}) copy-start(bf16[2,512,512]{2,1,0:T(8,128)(2,1)} %constant.13.clone.refs_3_) | copy-start | bytes 3145732
  45.6 6.8 %copy-start.1 = (bf16[2,2,256,1024]{3,2,1,0:T(8,128)(2,1)S(1)}, bf16[2,2,256,1024]{3,2,1,0:T(8,128)(2,1)}, u32[]{:S(2)}) copy-start(bf16[2,2,256,1024]{3,2,1,0:T(8,128)(2,1)} %constant.14.clone.backward_hbm) | copy-start | bytes 6291460
  45.7 6.7 %collective-permute-start = (bf16[512,128]{1,0:T(8,128)(2,1)S(1)}, bf16[512,128]{1,0:T(8,128)(2,1)S(1)}, u32[]{:S(2)}, u32[]{:S(2)}) collective-permute-start(bf16[512,128]{1,0:T(8,128)(2,1)S(1)} %bitcast.13), channel_id=1, source_target_pairs={{0,1},{1,0},{2,3},{3,2},{4,5},{5,4},{6,7},{7,6},{8,9},{9,8},{10,11... | collective-permute-start | bytes 393224 | tf_op jit(solution)/shard_map/signal_swap/ppermute | solution.py:270
  52.5 16.7 %copy-start.8 = (f32[256]{0:T(256)S(1)}, f32[256]{0:T(256)}, u32[]{:S(2)}) copy-start(f32[256]{0:T(256)} %param.14) | copy-start | bytes 3076
  52.5 28.8 %copy-start.3 = (bf16[256,256]{1,0:T(8,128)(2,1)S(1)}, bf16[256,256]{1,0:T(8,128)(2,1)}, u32[]{:S(2)}) copy-start(bf16[256,256]{1,0:T(8,128)(2,1)} %k_ref.1) | copy-start | bytes 393220
  52.5 28.8 %copy-start.4 = (bf16[256,256]{1,0:T(8,128)(2,1)S(1)}, bf16[256,256]{1,0:T(8,128)(2,1)}, u32[]{:S(2)}) copy-start(bf16[256,256]{1,0:T(8,128)(2,1)} %v_ref.1) | copy-start | bytes 393220
  52.5 28.8 %copy-start.6 = (bf16[256,256]{1,0:T(8,128)(2,1)S(1)}, bf16[256,256]{1,0:T(8,128)(2,1)}, u32[]{:S(2)}) copy-start(bf16[256,256]{1,0:T(8,128)(2,1)} %q_ref.1) | copy-start | bytes 393220
  55.9 3.4 %collective-permute-start.1 = (f32[256,256]{1,0:T(8,128)S(1)}, f32[256,256]{1,0:T(8,128)S(1)}, u32[]{:S(2)}, u32[]{:S(2)}) collective-permute-start(f32[256,256]{1,0:T(8,128)S(1)} %get-tuple-element.42), channel_id=1, source_target_pairs={{0,1},{1,0},{2,3},{3,2},{4,5},{5,4},{6,7},{7,6},{8,9},{9,8},{10,11... | collective-permute-start | bytes 786440 | tf_op jit(solution)/shard_map/result_swap/ppermute | solution.py:285
  60.1 21.2 %all-to-all-start.1 = ((bf16[256,1,2,128]{3,2,1,0:T(2,128)(2,1)}), bf16[256,1,2,128]{3,2,1,0:T(2,128)(2,1)S(1)}, u32[]{:S(2)}, u32[]{:S(2)}) async-start(bf16[256,1,2,128]{3,2,1,0:T(2,128)(2,1)} %bitcast.5), calls=%async_computation.1 | async-start | bytes 262144 | tf_op jit(solution)/shard_map/to_positions/all_to_all | solution.py:243

commit v2 on v1

--- a/solution.py
+++ b/solution.py
@@ -26,18 +26,24 @@
     return 2.0 * math.pi / denom * (numer % denom).astype(np.float64)
 
 
+def group_order(groups, rows):
+    halves = rows // 2
+    group_list = [(groups // 4 - i) % groups for i in range(groups)]
+    half_list = [(13 * halves // 16 - i) % halves for i in range(halves)]
+    return group_list, half_list
+
+
 @functools.lru_cache
 def tables(groups, rows, length):
     blocks, padded = groups * rows, 2 * groups * rows * length
-    pair = np.arange(blocks // 2, dtype=np.int64)
-    group, half_row = pair // (rows // 2), pair % (rows // 2)
+    group_list, half_list = (np.array(t, np.int64) for t in group_order(groups, rows))
     inner = np.arange(length, dtype=np.int64)
     forward, backward, fine, coarse = [], [], [], []
     for core in range(2):
-        low_parts = (2 * np.arange(groups)[None, :] + np.arange(2)[:, None]).reshape(-1)
-        high_parts = 2 * groups * (2 * np.arange(rows // 2) + core)
+        low_parts = (2 * group_list[None, :] + np.arange(2)[:, None]).reshape(-1)
+        high_parts = 2 * groups * (2 * half_list + core)
         low = (low_parts[:, None] + high_parts[None, :]).reshape(-1)
-        outer = group * rows + 2 * half_row + core
+        outer = (group_list[:, None] * rows + 2 * half_list[None, :] + core).reshape(-1)
         theta = unit_angles(low[:, None] * outer[None, :], 2 * blocks)
         matrix = np.concatenate([np.cos(theta), -np.sin(theta)], axis=0)
         forward.append(np.stack(split_bf16(matrix)))
@@ -234,7 +240,8 @@
     channels, length = q_proj.shape
     groups, rows = lax.axis_size("grp"), lax.axis_size("row")
     pairs = groups * rows // 2
-    same_core = [list(range(c, groups * rows, 2)) for c in range(2)]
+    group_list, half_list = group_order(groups, rows)
+    same_core = [[g * rows + 2 * i + c for g in group_list for i in half_list] for c in range(2)]
     swap = [(i, i ^ 1) for i in range(rows)]
     f32, bf16 = jnp.float32, jnp.bfloat16
     shape = jax.ShapeDtypeStruct

time: 82.8 us -> 75.5 us (0.912)
  waiting for transfers between devices: 30.3 us -> 15.7 us
  starting transfers between devices: 40.4 us -> 47.9 us
    all_to_all x2, waiting for transfers between devices: 28.9 us -> 14.3 us  [exchange(): lax.all_to_all(tensor.reshape(pairs, pieces, 2, LANES), both_axes, 0, 0,...]
    all_to_all x2, starting transfers between devices: 32.4 us -> 42 us  [exchange(): lax.all_to_all(tensor.reshape(pairs, pieces, 2, LANES), both_axes, 0, 0,...]
    ppermute x1, starting transfers between devices: 5.77 us -> 3.58 us  [body(): other = lax.ppermute(incoming[:, 4].reshape(2 * pairs, LANES), 'row', swap)]
where the time goes in v2:
time: 75.5 us; the launch traced here: 75 us
  starting transfers between devices  47.9 us (63%)
  waiting for transfers between devices  15.7 us (21%)
  Pallas kernels  8.18 us (11%)
  local copies, waits for them, and re-layouts  3.06 us (4%)
    all_to_all x2, starting transfers between devices, exchange(): lax.all_to_all(tensor.reshape(pairs, pieces, 2, LANES), both_axes, 0, 0,...  42 us
    all_to_all x2, waiting for transfers between devices, exchange(): lax.all_to_all(tensor.reshape(pairs, pieces, 2, LANES), both_axes, 0, 0,...  14.3 us
    ppermute x1, starting transfers between devices, body(): other = lax.ppermute(incoming[:, 4].reshape(2 * pairs, LANES), 'row', swap)  3.58 us
    pallas_call x1, Pallas kernels, body(): call(spectrum_kernel, [shape((pairs, length), f32)] * 2, [pltpu.VMEM((2 *...  3.43 us
    unnamed x18, local copies, waits for them, and re-layouts  2.84 us
    ppermute x1, starting transfers between devices, body(): came = lax.ppermute(sent, 'row', swap)  2.27 us
    pallas_call x1, Pallas kernels, body(): call(pack_kernel, shape((10 * channels, LANES), bf16), [pltpu.VMEM((chann...  2.15 us
  transfers between devices with their start and end apart: 4, of which 4 were waited for; matrix products, arithmetic and copies ran while one was open for 0% of the time, Pallas kernels for 1%

profile of v2, /device:TPU:1, one launch (start us, length us, event | category | flops | bytes accessed | tf_op | source)
XLA Modules:
  0.0 75.0 jit_solution(17171505521209842570)
XLA Ops:
  0.0 2.1 %pack.1 = bf16[2560,128]{1,0:T(8,128)(2,1)} custom-call(bf16[256,256]{1,0:T(8,128)(2,1)} %k_ref.1, bf16[256,256]{1,0:T(8,128)(2,1)} %v_ref.1, f32[4,512,128]{2,1,0:T(8,128)} %bitcast.12), custom_call_target="tpu_custom_call" | custom-call | tf_op jit(solution)/shard_map/pack/pallas_call | solution.py:256
  2.2 25.1 %all-to-all-start = ((bf16[256,5,2,128]{3,2,1,0:T(2,128)(2,1)}), bf16[256,5,2,128]{3,2,1,0:T(2,128)(2,1)S(1)}, u32[]{:S(2)}, u32[]{:S(2)}) async-start(bf16[256,5,2,128]{3,2,1,0:T(2,128)(2,1)} %bitcast.11), calls=%async_computation | async-start | bytes 1310720 | tf_op jit(solution)/shard_map/to_channels/all_to_all | solution.py:250
  27.3 0.0 copy-done.5
  27.3 0.0 copy-done.7
  27.3 0.0 copy-start
  27.3 1.6 %copy-done = bf16[2,2,1024,256]{3,2,1,0:T(8,128)(2,1)S(1)} copy-done((bf16[2,2,1024,256]{3,2,1,0:T(8,128)(2,1)S(1)}, bf16[2,2,1024,256]{3,2,1,0:T(8,128)(2,1)}, u32[]{:S(2)}) %copy-start) | copy-done | bytes 2097176
  28.9 1.2 %copy-done.2 = bf16[2,512,512]{2,1,0:T(8,128)(2,1)S(1)} copy-done((bf16[2,512,512]{2,1,0:T(8,128)(2,1)S(1)}, bf16[2,512,512]{2,1,0:T(8,128)(2,1)}, u32[]{:S(2)}) %copy-start.2) | copy-done | bytes 1048600
  30.1 0.4 tables.1
  30.5 11.0 %all-to-all-done = bf16[256,5,2,128]{3,2,1,0:T(2,128)(2,1)S(1)} async-done(((bf16[256,5,2,128]{3,2,1,0:T(2,128)(2,1)}), bf16[256,5,2,128]{3,2,1,0:T(2,128)(2,1)S(1)}, u32[]{:S(2)}, u32[]{:S(2)}) %all-to-all-start) | async-done | bytes 655392 | tf_op jit(solution)/shard_map/to_channels/all_to_all | solution.py:250
  41.5 0.1 slice.3
  41.6 3.6 %collective-permute-start = (bf16[512,128]{1,0:T(8,128)(2,1)S(1)}, bf16[512,128]{1,0:T(8,128)(2,1)S(1)}, u32[]{:S(2)}, u32[]{:S(2)}) collective-permute-start(bf16[512,128]{1,0:T(8,128)(2,1)S(1)} %bitcast.13), channel_id=1, source_target_pairs={{0,1},{1,0},{2,3},{3,2},{4,5},{5,4},{6,7},{7,6},{8,9},{9,8},{10,11... | collective-permute-start | bytes 393224 | tf_op jit(solution)/shard_map/signal_swap/ppermute | solution.py:277
  45.2 0.7 own_positions.1
  45.9 0.2 collective-permute-done.other_ref
  46.1 0.0 copy-done.1
  46.2 0.0 copy-start.6
  46.2 3.4 %spectrum.1 = (f32[256,256]{1,0:T(8,128)S(1)}, f32[256,256]{1,0:T(8,128)S(1)}) custom-call(bf16[2,2,256,1024]{3,2,1,0:T(8,128)(2,1)S(1)} %copy-done.1, bf16[512,128]{1,0:T(8,128)(2,1)S(1)} %collective-permute-done.other_ref, bf16[2,1024,256]{2,1,0:T(8,128)(2,1)S(1)} %get-tuple-element.34.forward_ref, f32[1024,256]{1,0:T(8,128)S(1)} %get-tuple-element.37.field_ref, ...), custom_call_target="tpu_custom_call" | custom-call | tf_op jit(solution)/shard_map/spectrum/pallas_call | solution.py:286
  49.6 2.3 %collective-permute-start.1 = (f32[256,256]{1,0:T(8,128)S(1)}, f32[256,256]{1,0:T(8,128)S(1)}, u32[]{:S(2)}, u32[]{:S(2)}) collective-permute-start(f32[256,256]{1,0:T(8,128)S(1)} %get-tuple-element.42), channel_id=1, source_target_pairs={{0,1},{1,0},{2,3},{3,2},{4,5},{5,4},{6,7},{7,6},{8,9},{9,8},{10,11... | collective-permute-start | bytes 786440 | tf_op jit(solution)/shard_map/result_swap/ppermute | solution.py:292
  51.9 1.1 %collective-permute-done.1.came_ref = f32[256,256]{1,0:T(8,128)S(1)} collective-permute-done((f32[256,256]{1,0:T(8,128)S(1)}, f32[256,256]{1,0:T(8,128)S(1)}, u32[]{:S(2)}, u32[]{:S(2)}) %collective-permute-start.1) | collective-permute-done | bytes 262176 | tf_op jit(solution)/shard_map/result_swap/ppermute | solution.py:292
  53.0 0.7 add_cores.1
  53.7 16.9 %all-to-all-start.1 = ((bf16[256,1,2,128]{3,2,1,0:T(2,128)(2,1)}), bf16[256,1,2,128]{3,2,1,0:T(2,128)(2,1)S(1)}, u32[]{:S(2)}, u32[]{:S(2)}) async-start(bf16[256,1,2,128]{3,2,1,0:T(2,128)(2,1)} %bitcast.5), calls=%async_computation.1 | async-start | bytes 262144 | tf_op jit(solution)/shard_map/to_positions/all_to_all | solution.py:250
  70.7 0.0 copy-done.8
  70.7 0.1 copy.17.gain_ref
  70.8 3.3 %all-to-all-done.1 = bf16[256,1,2,128]{3,2,1,0:T(2,128)(2,1)S(1)} async-done(((bf16[256,1,2,128]{3,2,1,0:T(2,128)(2,1)}), bf16[256,1,2,128]{3,2,1,0:T(2,128)(2,1)S(1)}, u32[]{:S(2)}, u32[]{:S(2)}) %all-to-all-start.1) | async-done | bytes 131104 | tf_op jit(solution)/shard_map/to_positions/all_to_all | solution.py:250
  74.1 0.8 %gate.1 = f32[256,256]{1,0:T(8,128)} custom-call(bf16[512,128]{1,0:T(8,128)(2,1)S(1)} %bitcast.10, bf16[256,256]{1,0:T(8,128)(2,1)S(1)} %copy-done.6, bf16[256,256]{1,0:T(8,128)(2,1)S(1)} %copy-done.3, bf16[256,256]{1,0:T(8,128)(2,1)S(1)} %copy-done.4, f32[256,1]{1,0:T(8,128)S(1)} %copy.17.gain_ref), custom_call_target="tpu_custom_call" | custom-call | tf_op jit(solution)/shard_map/gate/pallas_call | solution.py:300
  (10 shorter events, 0.0 us)
Async XLA Ops:
  0.0 27.3 %copy-start.5 = (f32[2,2,32,384]{3,2,1,0:T(8,128)S(1)}, f32[2,2,32,384]{3,2,1,0:T(8,128)}, u32[]{:S(2)}) copy-start(f32[2,2,32,384]{3,2,1,0:T(8,128)} %constant.11.clone.refs_1_) | copy-start | bytes 589828
  0.0 27.3 %copy-start.7 = (f32[2,2,16,384]{3,2,1,0:T(8,128)S(1)}, f32[2,2,16,384]{3,2,1,0:T(8,128)}, u32[]{:S(2)}) copy-start(f32[2,2,16,384]{3,2,1,0:T(8,128)} %constant.12.clone.refs_2_) | copy-start | bytes 294916
  2.2 39.3 %all-to-all-start = ((bf16[256,5,2,128]{3,2,1,0:T(2,128)(2,1)}), bf16[256,5,2,128]{3,2,1,0:T(2,128)(2,1)S(1)}, u32[]{:S(2)}, u32[]{:S(2)}) async-start(bf16[256,5,2,128]{3,2,1,0:T(2,128)(2,1)} %bitcast.11), calls=%async_computation | async-start | bytes 1310720 | tf_op jit(solution)/shard_map/to_channels/all_to_all | solution.py:250
  27.3 1.6 %copy-start = (bf16[2,2,1024,256]{3,2,1,0:T(8,128)(2,1)S(1)}, bf16[2,2,1024,256]{3,2,1,0:T(8,128)(2,1)}, u32[]{:S(2)}) copy-start(bf16[2,2,1024,256]{3,2,1,0:T(8,128)(2,1)} %constant.10.clone.refs_0_) | copy-start | bytes 6291460
  28.9 1.2 %copy-start.2 = (bf16[2,512,512]{2,1,0:T(8,128)(2,1)S(1)}, bf16[2,512,512]{2,1,0:T(8,128)(2,1)}, u32[]{:S(2)}) copy-start(bf16[2,512,512]{2,1,0:T(8,128)(2,1)} %constant.13.clone.refs_3_) | copy-start | bytes 3145732
  41.5 4.7 %copy-start.1 = (bf16[2,2,256,1024]{3,2,1,0:T(8,128)(2,1)S(1)}, bf16[2,2,256,1024]{3,2,1,0:T(8,128)(2,1)}, u32[]{:S(2)}) copy-start(bf16[2,2,256,1024]{3,2,1,0:T(8,128)(2,1)} %constant.14.clone.backward_hbm) | copy-start | bytes 6291460
  41.6 4.6 %collective-permute-start = (bf16[512,128]{1,0:T(8,128)(2,1)S(1)}, bf16[512,128]{1,0:T(8,128)(2,1)S(1)}, u32[]{:S(2)}, u32[]{:S(2)}) collective-permute-start(bf16[512,128]{1,0:T(8,128)(2,1)S(1)} %bitcast.13), channel_id=1, source_target_pairs={{0,1},{1,0},{2,3},{3,2},{4,5},{5,4},{6,7},{7,6},{8,9},{9,8},{10,11... | collective-permute-start | bytes 393224 | tf_op jit(solution)/shard_map/signal_swap/ppermute | solution.py:277
  46.1 24.5 %copy-start.8 = (f32[256]{0:T(256)S(1)}, f32[256]{0:T(256)}, u32[]{:S(2)}) copy-start(f32[256]{0:T(256)} %param.14) | copy-start | bytes 3076
  46.2 28.0 %copy-start.3 = (bf16[256,256]{1,0:T(8,128)(2,1)S(1)}, bf16[256,256]{1,0:T(8,128)(2,1)}, u32[]{:S(2)}) copy-start(bf16[256,256]{1,0:T(8,128)(2,1)} %k_ref.1) | copy-start | bytes 393220
  46.2 28.0 %copy-start.4 = (bf16[256,256]{1,0:T(8,128)(2,1)S(1)}, bf16[256,256]{1,0:T(8,128)(2,1)}, u32[]{:S(2)}) copy-start(bf16[256,256]{1,0:T(8,128)(2,1)} %v_ref.1) | copy-start | bytes 393220
  46.2 28.0 %copy-start.6 = (bf16[256,256]{1,0:T(8,128)(2,1)S(1)}, bf16[256,256]{1,0:T(8,128)(2,1)}, u32[]{:S(2)}) copy-start(bf16[256,256]{1,0:T(8,128)(2,1)} %q_ref.1) | copy-start | bytes 393220
  49.6 3.4 %collective-permute-start.1 = (f32[256,256]{1,0:T(8,128)S(1)}, f32[256,256]{1,0:T(8,128)S(1)}, u32[]{:S(2)}, u32[]{:S(2)}) collective-permute-start(f32[256,256]{1,0:T(8,128)S(1)} %get-tuple-element.42), channel_id=1, source_target_pairs={{0,1},{1,0},{2,3},{3,2},{4,5},{5,4},{6,7},{7,6},{8,9},{9,8},{10,11... | collective-permute-start | bytes 786440 | tf_op jit(solution)/shard_map/result_swap/ppermute | solution.py:292
  53.7 20.4 %all-to-all-start.1 = ((bf16[256,1,2,128]{3,2,1,0:T(2,128)(2,1)}), bf16[256,1,2,128]{3,2,1,0:T(2,128)(2,1)S(1)}, u32[]{:S(2)}, u32[]{:S(2)}) async-start(bf16[256,1,2,128]{3,2,1,0:T(2,128)(2,1)} %bitcast.5), calls=%async_computation.1 | async-start | bytes 262144 | tf_op jit(solution)/shard_map/to_positions/all_to_all | solution.py:250

commit v3 on v2

--- a/solution.py
+++ b/solution.py
@@ -27,10 +27,19 @@
 
 
 def group_order(groups, rows):
-    halves = rows // 2
-    group_list = [(groups // 4 - i) % groups for i in range(groups)]
-    half_list = [(13 * halves // 16 - i) % halves for i in range(halves)]
-    return group_list, half_list
+    ring, halves = groups // 2, rows // 2
+    first_group, first_half = groups // 4, 13 * halves // 16
+
+    def nearness(group):
+        place = group % ring
+        return min(place, ring - place), place, group
+
+    group_list = sorted((g for g in range(groups) if g != first_group), key=nearness)
+    half_list = sorted(
+        (i for i in range(halves) if i != first_half),
+        key=lambda i: (-(i % (halves // 2)), -i),
+    )
+    return [first_group, *group_list], [first_half, *half_list]
 
 
 @functools.lru_cache

time: 75.5 us -> 75.4 us (level)
  no operation moved by 1% of the time
where the time goes in v3:
time: 75.4 us; the launch traced here: 74.9 us
  starting transfers between devices  47.7 us (63%)
  waiting for transfers between devices  15.8 us (21%)
  Pallas kernels  8.17 us (11%)
  local copies, waits for them, and re-layouts  3.06 us (4%)
    all_to_all x2, starting transfers between devices, exchange(): lax.all_to_all(tensor.reshape(pairs, pieces, 2, LANES), both_axes, 0, 0,...  41.4 us
    all_to_all x2, waiting for transfers between devices, exchange(): lax.all_to_all(tensor.reshape(pairs, pieces, 2, LANES), both_axes, 0, 0,...  14.4 us
    ppermute x1, starting transfers between devices, body(): other = lax.ppermute(incoming[:, 4].reshape(2 * pairs, LANES), 'row', swap)  3.99 us
    pallas_call x1, Pallas kernels, body(): call(spectrum_kernel, [shape((pairs, length), f32)] * 2, [pltpu.VMEM((2 *...  3.43 us
    unnamed x18, local copies, waits for them, and re-layouts  2.84 us
    ppermute x1, starting transfers between devices, body(): came = lax.ppermute(sent, 'row', swap)  2.28 us
    pallas_call x1, Pallas kernels, body(): call(pack_kernel, shape((10 * channels, LANES), bf16), [pltpu.VMEM((chann...  2.15 us
  transfers between devices with their start and end apart: 4, of which 4 were waited for; matrix products, arithmetic and copies ran while one was open for 0% of the time, Pallas kernels for 1%

profile of v3, /device:TPU:1, one launch (start us, length us, event | category | flops | bytes accessed | tf_op | source)
XLA Modules:
  0.0 74.9 jit_solution(235238032431700914)
XLA Ops:
  0.0 2.1 %pack.1 = bf16[2560,128]{1,0:T(8,128)(2,1)} custom-call(bf16[256,256]{1,0:T(8,128)(2,1)} %k_ref.1, bf16[256,256]{1,0:T(8,128)(2,1)} %v_ref.1, f32[4,512,128]{2,1,0:T(8,128)} %bitcast.12), custom_call_target="tpu_custom_call" | custom-call | tf_op jit(solution)/shard_map/pack/pallas_call | solution.py:265
  2.2 24.8 %all-to-all-start = ((bf16[256,5,2,128]{3,2,1,0:T(2,128)(2,1)}), bf16[256,5,2,128]{3,2,1,0:T(2,128)(2,1)S(1)}, u32[]{:S(2)}, u32[]{:S(2)}) async-start(bf16[256,5,2,128]{3,2,1,0:T(2,128)(2,1)} %bitcast.11), calls=%async_computation | async-start | bytes 1310720 | tf_op jit(solution)/shard_map/to_channels/all_to_all | solution.py:259
  27.0 0.0 copy-done.5
  27.0 0.0 copy-done.7
  27.0 0.0 copy-start
  27.0 1.6 %copy-done = bf16[2,2,1024,256]{3,2,1,0:T(8,128)(2,1)S(1)} copy-done((bf16[2,2,1024,256]{3,2,1,0:T(8,128)(2,1)S(1)}, bf16[2,2,1024,256]{3,2,1,0:T(8,128)(2,1)}, u32[]{:S(2)}) %copy-start) | copy-done | bytes 2097176
  28.6 1.2 %copy-done.2 = bf16[2,512,512]{2,1,0:T(8,128)(2,1)S(1)} copy-done((bf16[2,512,512]{2,1,0:T(8,128)(2,1)S(1)}, bf16[2,512,512]{2,1,0:T(8,128)(2,1)}, u32[]{:S(2)}) %copy-start.2) | copy-done | bytes 1048600
  29.8 0.4 tables.1
  30.2 11.0 %all-to-all-done = bf16[256,5,2,128]{3,2,1,0:T(2,128)(2,1)S(1)} async-done(((bf16[256,5,2,128]{3,2,1,0:T(2,128)(2,1)}), bf16[256,5,2,128]{3,2,1,0:T(2,128)(2,1)S(1)}, u32[]{:S(2)}, u32[]{:S(2)}) %all-to-all-start) | async-done | bytes 655392 | tf_op jit(solution)/shard_map/to_channels/all_to_all | solution.py:259
  41.1 0.1 slice.3
  41.2 4.0 %collective-permute-start = (bf16[512,128]{1,0:T(8,128)(2,1)S(1)}, bf16[512,128]{1,0:T(8,128)(2,1)S(1)}, u32[]{:S(2)}, u32[]{:S(2)}) collective-permute-start(bf16[512,128]{1,0:T(8,128)(2,1)S(1)} %bitcast.13), channel_id=1, source_target_pairs={{0,1},{1,0},{2,3},{3,2},{4,5},{5,4},{6,7},{7,6},{8,9},{9,8},{10,11... | collective-permute-start | bytes 393224 | tf_op jit(solution)/shard_map/signal_swap/ppermute | solution.py:286
  45.2 0.7 own_positions.1
  46.0 0.2 collective-permute-done.other_ref
  46.2 0.0 copy-done.1
  46.2 0.0 copy-start.6
  46.2 3.4 %spectrum.1 = (f32[256,256]{1,0:T(8,128)S(1)}, f32[256,256]{1,0:T(8,128)S(1)}) custom-call(bf16[2,2,256,1024]{3,2,1,0:T(8,128)(2,1)S(1)} %copy-done.1, bf16[512,128]{1,0:T(8,128)(2,1)S(1)} %collective-permute-done.other_ref, bf16[2,1024,256]{2,1,0:T(8,128)(2,1)S(1)} %get-tuple-element.34.forward_ref, f32[1024,256]{1,0:T(8,128)S(1)} %get-tuple-element.37.field_ref, ...), custom_call_target="tpu_custom_call" | custom-call | tf_op jit(solution)/shard_map/spectrum/pallas_call | solution.py:295
  49.7 2.3 %collective-permute-start.1 = (f32[256,256]{1,0:T(8,128)S(1)}, f32[256,256]{1,0:T(8,128)S(1)}, u32[]{:S(2)}, u32[]{:S(2)}) collective-permute-start(f32[256,256]{1,0:T(8,128)S(1)} %get-tuple-element.42), channel_id=1, source_target_pairs={{0,1},{1,0},{2,3},{3,2},{4,5},{5,4},{6,7},{7,6},{8,9},{9,8},{10,11... | collective-permute-start | bytes 786440 | tf_op jit(solution)/shard_map/result_swap/ppermute | solution.py:301
  51.9 1.1 %collective-permute-done.1.came_ref = f32[256,256]{1,0:T(8,128)S(1)} collective-permute-done((f32[256,256]{1,0:T(8,128)S(1)}, f32[256,256]{1,0:T(8,128)S(1)}, u32[]{:S(2)}, u32[]{:S(2)}) %collective-permute-start.1) | collective-permute-done | bytes 262176 | tf_op jit(solution)/shard_map/result_swap/ppermute | solution.py:301
  53.1 0.7 add_cores.1
  53.8 16.6 %all-to-all-start.1 = ((bf16[256,1,2,128]{3,2,1,0:T(2,128)(2,1)}), bf16[256,1,2,128]{3,2,1,0:T(2,128)(2,1)S(1)}, u32[]{:S(2)}, u32[]{:S(2)}) async-start(bf16[256,1,2,128]{3,2,1,0:T(2,128)(2,1)} %bitcast.5), calls=%async_computation.1 | async-start | bytes 262144 | tf_op jit(solution)/shard_map/to_positions/all_to_all | solution.py:259
  70.4 0.1 copy.17.gain_ref
  70.6 3.5 %all-to-all-done.1 = bf16[256,1,2,128]{3,2,1,0:T(2,128)(2,1)S(1)} async-done(((bf16[256,1,2,128]{3,2,1,0:T(2,128)(2,1)}), bf16[256,1,2,128]{3,2,1,0:T(2,128)(2,1)S(1)}, u32[]{:S(2)}, u32[]{:S(2)}) %all-to-all-start.1) | async-done | bytes 131104 | tf_op jit(solution)/shard_map/to_positions/all_to_all | solution.py:259
  74.1 0.0 copy-done.3
  74.1 0.8 %gate.1 = f32[256,256]{1,0:T(8,128)} custom-call(bf16[512,128]{1,0:T(8,128)(2,1)S(1)} %bitcast.10, bf16[256,256]{1,0:T(8,128)(2,1)S(1)} %copy-done.6, bf16[256,256]{1,0:T(8,128)(2,1)S(1)} %copy-done.3, bf16[256,256]{1,0:T(8,128)(2,1)S(1)} %copy-done.4, f32[256,1]{1,0:T(8,128)S(1)} %copy.17.gain_ref), custom_call_target="tpu_custom_call" | custom-call | tf_op jit(solution)/shard_map/gate/pallas_call | solution.py:309
  (10 shorter events, 0.0 us)
Async XLA Ops:
  0.0 27.0 %copy-start.5 = (f32[2,2,32,384]{3,2,1,0:T(8,128)S(1)}, f32[2,2,32,384]{3,2,1,0:T(8,128)}, u32[]{:S(2)}) copy-start(f32[2,2,32,384]{3,2,1,0:T(8,128)} %constant.11.clone.refs_1_) | copy-start | bytes 589828
  0.0 27.0 %copy-start.7 = (f32[2,2,16,384]{3,2,1,0:T(8,128)S(1)}, f32[2,2,16,384]{3,2,1,0:T(8,128)}, u32[]{:S(2)}) copy-start(f32[2,2,16,384]{3,2,1,0:T(8,128)} %constant.12.clone.refs_2_) | copy-start | bytes 294916
  2.2 39.0 %all-to-all-start = ((bf16[256,5,2,128]{3,2,1,0:T(2,128)(2,1)}), bf16[256,5,2,128]{3,2,1,0:T(2,128)(2,1)S(1)}, u32[]{:S(2)}, u32[]{:S(2)}) async-start(bf16[256,5,2,128]{3,2,1,0:T(2,128)(2,1)} %bitcast.11), calls=%async_computation | async-start | bytes 1310720 | tf_op jit(solution)/shard_map/to_channels/all_to_all | solution.py:259
  27.0 1.6 %copy-start = (bf16[2,2,1024,256]{3,2,1,0:T(8,128)(2,1)S(1)}, bf16[2,2,1024,256]{3,2,1,0:T(8,128)(2,1)}, u32[]{:S(2)}) copy-start(bf16[2,2,1024,256]{3,2,1,0:T(8,128)(2,1)} %constant.10.clone.refs_0_) | copy-start | bytes 6291460
  28.6 1.2 %copy-start.2 = (bf16[2,512,512]{2,1,0:T(8,128)(2,1)S(1)}, bf16[2,512,512]{2,1,0:T(8,128)(2,1)}, u32[]{:S(2)}) copy-start(bf16[2,512,512]{2,1,0:T(8,128)(2,1)} %constant.13.clone.refs_3_) | copy-start | bytes 3145732
  41.1 5.1 %copy-start.1 = (bf16[2,2,256,1024]{3,2,1,0:T(8,128)(2,1)S(1)}, bf16[2,2,256,1024]{3,2,1,0:T(8,128)(2,1)}, u32[]{:S(2)}) copy-start(bf16[2,2,256,1024]{3,2,1,0:T(8,128)(2,1)} %constant.14.clone.backward_hbm) | copy-start | bytes 6291460
  41.2 5.0 %collective-permute-start = (bf16[512,128]{1,0:T(8,128)(2,1)S(1)}, bf16[512,128]{1,0:T(8,128)(2,1)S(1)}, u32[]{:S(2)}, u32[]{:S(2)}) collective-permute-start(bf16[512,128]{1,0:T(8,128)(2,1)S(1)} %bitcast.13), channel_id=1, source_target_pairs={{0,1},{1,0},{2,3},{3,2},{4,5},{5,4},{6,7},{7,6},{8,9},{9,8},{10,11... | collective-permute-start | bytes 393224 | tf_op jit(solution)/shard_map/signal_swap/ppermute | solution.py:286
  46.2 24.2 %copy-start.8 = (f32[256]{0:T(256)S(1)}, f32[256]{0:T(256)}, u32[]{:S(2)}) copy-start(f32[256]{0:T(256)} %param.14) | copy-start | bytes 3076
  46.2 27.9 %copy-start.3 = (bf16[256,256]{1,0:T(8,128)(2,1)S(1)}, bf16[256,256]{1,0:T(8,128)(2,1)}, u32[]{:S(2)}) copy-start(bf16[256,256]{1,0:T(8,128)(2,1)} %k_ref.1) | copy-start | bytes 393220
  46.2 27.9 %copy-start.4 = (bf16[256,256]{1,0:T(8,128)(2,1)S(1)}, bf16[256,256]{1,0:T(8,128)(2,1)}, u32[]{:S(2)}) copy-start(bf16[256,256]{1,0:T(8,128)(2,1)} %v_ref.1) | copy-start | bytes 393220
  46.2 27.9 %copy-start.6 = (bf16[256,256]{1,0:T(8,128)(2,1)S(1)}, bf16[256,256]{1,0:T(8,128)(2,1)}, u32[]{:S(2)}) copy-start(bf16[256,256]{1,0:T(8,128)(2,1)} %q_ref.1) | copy-start | bytes 393220
  49.7 3.4 %collective-permute-start.1 = (f32[256,256]{1,0:T(8,128)S(1)}, f32[256,256]{1,0:T(8,128)S(1)}, u32[]{:S(2)}, u32[]{:S(2)}) collective-permute-start(f32[256,256]{1,0:T(8,128)S(1)} %get-tuple-element.42), channel_id=1, source_target_pairs={{0,1},{1,0},{2,3},{3,2},{4,5},{5,4},{6,7},{7,6},{8,9},{9,8},{10,11... | collective-permute-start | bytes 786440 | tf_op jit(solution)/shard_map/result_swap/ppermute | solution.py:301
  53.8 20.3 %all-to-all-start.1 = ((bf16[256,1,2,128]{3,2,1,0:T(2,128)(2,1)}), bf16[256,1,2,128]{3,2,1,0:T(2,128)(2,1)S(1)}, u32[]{:S(2)}, u32[]{:S(2)}) async-start(bf16[256,1,2,128]{3,2,1,0:T(2,128)(2,1)} %bitcast.5), calls=%async_computation.1 | async-start | bytes 262144 | tf_op jit(solution)/shard_map/to_positions/all_to_all | solution.py:259

commit v4 on v3

--- a/solution.py
+++ b/solution.py
@@ -13,6 +13,7 @@
 both_axes = ("grp", "row")
 LANES = 128
 CHUNKS = 4
+SPARE = 16
 
 
 def split_bf16(table):
@@ -153,7 +154,7 @@
 
 def own_kernel(got_ref, forward_ref, fine_ref, coarse_ref, field_ref, response_ref, twist_ref, wide):
     pairs = got_ref.shape[0] // 10
-    wide[...] = got_ref[...].astype(jnp.float32)
+    wide[: got_ref.shape[0], :] = got_ref[...].astype(jnp.float32)
     signal = joined(wide, 8, 10, pairs).astype(jnp.bfloat16)
     field_ref[...] = dot(forward_ref[0], signal) + dot(forward_ref[1], signal)
     for part in range(2):
@@ -179,7 +180,7 @@
     fetch.start()
     pairs = other_ref.shape[0] // 2
     count, length = 2 * pairs, 2 * LANES
-    wide[...] = other_ref[...].astype(jnp.float32)
+    wide[: other_ref.shape[0], :] = other_ref[...].astype(jnp.float32)
     signal = joined(wide, 0, 2, pairs).astype(jnp.bfloat16)
     field = dot(forward_ref[0], signal) + dot(forward_ref[1], signal)
     shift_cos = jnp.concatenate([twist_ref[0, :, length:]] * 2, axis=1)
@@ -216,12 +217,12 @@
     conv = kept_ref[...] + came_ref[...]
     for half in range(2):
         wide[pl.ds(half, pairs, stride=2), :] = conv[:, half * LANES : (half + 1) * LANES]
-    out_ref[...] = wide[...].astype(jnp.bfloat16)
+    out_ref[...] = wide[: out_ref.shape[0], :].astype(jnp.bfloat16)
 
 
 def gate_kernel(got_ref, q_ref, k_ref, v_ref, gain_ref, out_ref, wide):
     channels = q_ref.shape[0]
-    wide[...] = got_ref[...].astype(jnp.float32)
+    wide[: got_ref.shape[0], :] = got_ref[...].astype(jnp.float32)
     conv = joined(wide, 0, 2, channels)
     signal = (k_ref[...].astype(jnp.float32) * v_ref[...].astype(jnp.float32)).astype(jnp.bfloat16)
     out_ref[...] = q_ref[...].astype(jnp.float32) * (
@@ -265,7 +266,8 @@
         outgoing = call(
             pack_kernel, shape((10 * channels, LANES), bf16),
             [pltpu.VMEM((channels, length), bf16)] * 2
-            + [pltpu.VMEM((4, 2 * channels, LANES), f32), pltpu.VMEM((10 * channels, LANES), f32),
+            + [pltpu.VMEM((4, 2 * channels + SPARE, LANES), f32),
+               pltpu.VMEM((10 * channels + SPARE, LANES), f32),
                pltpu.VMEM((10 * channels, LANES), bf16), pltpu.SemaphoreType.DMA((2 + 2 * CHUNKS,))],
             58, 3, True,
         )(k_proj, v_proj, filter_spectrum.reshape(4, 2 * channels, LANES))
@@ -289,26 +291,27 @@
             own_kernel,
             [shape((4 * pairs, length), f32), shape((2, 2 * pairs, length), f32),
              shape((2, 2 * pairs, length + LANES), f32)],
-            [pltpu.VMEM((10 * pairs, LANES), f32)], 8,
+            [pltpu.VMEM((10 * pairs + SPARE, LANES), f32)], 8,
         )(incoming.reshape(10 * pairs, LANES), forward, fine, coarse)
     with jax.named_scope("spectrum"):
         sent, kept = call(
             spectrum_kernel, [shape((pairs, length), f32)] * 2,
-            [pltpu.VMEM((2 * pairs, LANES), f32), pltpu.VMEM(backward.shape[1:], bf16),
+            [pltpu.VMEM((2 * pairs + SPARE, LANES), f32), pltpu.VMEM(backward.shape[1:], bf16),
              pltpu.SemaphoreType.DMA], 20, 1, operands=7,
         )(jnp.asarray(backward), other, forward, field, response, twist, mixed)
     with jax.named_scope("result_swap"):
         came = lax.ppermute(sent, "row", swap)
     with jax.named_scope("add_cores"):
         result = call(
-            add_kernel, shape((2 * pairs, LANES), bf16), [pltpu.VMEM((2 * pairs, LANES), f32)], 4
+            add_kernel, shape((2 * pairs, LANES), bf16),
+            [pltpu.VMEM((2 * pairs + SPARE, LANES), f32)], 4
         )(kept, came)
     with jax.named_scope("to_positions"):
         returned = exchange(result, 1)
     with jax.named_scope("gate"):
         return call(
             gate_kernel, shape((channels, length), f32),
-            [pltpu.VMEM((2 * channels, LANES), f32)], 4,
+            [pltpu.VMEM((2 * channels + SPARE, LANES), f32)], 4,
         )(returned.reshape(2 * channels, LANES), q_proj, k_proj, v_proj, skip_gain[:, None])
 
 

time: 75.4 us -> 75.4 us (level)
  no operation moved by 1% of the time
where the time goes in v4:
time: 75.4 us; the launch traced here: 74.9 us
  starting transfers between devices  47.7 us (63%)
  waiting for transfers between devices  15.8 us (21%)
  Pallas kernels  8.17 us (11%)
  local copies, waits for them, and re-layouts  3.06 us (4%)
    all_to_all x2, starting transfers between devices, exchange(): lax.all_to_all(tensor.reshape(pairs, pieces, 2, LANES), both_axes, 0, 0,...  41.4 us
    all_to_all x2, waiting for transfers between devices, exchange(): lax.all_to_all(tensor.reshape(pairs, pieces, 2, LANES), both_axes, 0, 0,...  14.4 us
    ppermute x1, starting transfers between devices, body(): other = lax.ppermute(incoming[:, 4].reshape(2 * pairs, LANES), 'row', swap)  3.99 us
    pallas_call x1, Pallas kernels, body(): call(spectrum_kernel, [shape((pairs, length), f32)] * 2, [pltpu.VMEM((2 *...  3.42 us
    unnamed x18, local copies, waits for them, and re-layouts  2.84 us
    ppermute x1, starting transfers between devices, body(): came = lax.ppermute(sent, 'row', swap)  2.28 us
    pallas_call x1, Pallas kernels, body(): call(pack_kernel, shape((10 * channels, LANES), bf16), [pltpu.VMEM((chann...  2.15 us
  transfers between devices with their start and end apart: 4, of which 4 were waited for; matrix products, arithmetic and copies ran while one was open for 0% of the time, Pallas kernels for 1%

profile of v4, /device:TPU:1, one launch (start us, length us, event | category | flops | bytes accessed | tf_op | source)
XLA Modules:
  0.0 74.9 jit_solution(1392284172745406951)
XLA Ops:
  0.0 2.1 %pack.1 = bf16[2560,128]{1,0:T(8,128)(2,1)} custom-call(bf16[256,256]{1,0:T(8,128)(2,1)} %k_ref.1, bf16[256,256]{1,0:T(8,128)(2,1)} %v_ref.1, f32[4,512,128]{2,1,0:T(8,128)} %bitcast.12), custom_call_target="tpu_custom_call" | custom-call | tf_op jit(solution)/shard_map/pack/pallas_call | solution.py:266
  2.2 24.8 %all-to-all-start = ((bf16[256,5,2,128]{3,2,1,0:T(2,128)(2,1)}), bf16[256,5,2,128]{3,2,1,0:T(2,128)(2,1)S(1)}, u32[]{:S(2)}, u32[]{:S(2)}) async-start(bf16[256,5,2,128]{3,2,1,0:T(2,128)(2,1)} %bitcast.11), calls=%async_computation | async-start | bytes 1310720 | tf_op jit(solution)/shard_map/to_channels/all_to_all | solution.py:260
  27.0 0.0 copy-done.5
  27.0 0.0 copy-done.7
  27.0 0.0 copy-start
  27.0 1.6 %copy-done = bf16[2,2,1024,256]{3,2,1,0:T(8,128)(2,1)S(1)} copy-done((bf16[2,2,1024,256]{3,2,1,0:T(8,128)(2,1)S(1)}, bf16[2,2,1024,256]{3,2,1,0:T(8,128)(2,1)}, u32[]{:S(2)}) %copy-start) | copy-done | bytes 2097176
  28.6 1.2 %copy-done.2 = bf16[2,512,512]{2,1,0:T(8,128)(2,1)S(1)} copy-done((bf16[2,512,512]{2,1,0:T(8,128)(2,1)S(1)}, bf16[2,512,512]{2,1,0:T(8,128)(2,1)}, u32[]{:S(2)}) %copy-start.2) | copy-done | bytes 1048600
  29.8 0.4 tables.1
  30.2 11.0 %all-to-all-done = bf16[256,5,2,128]{3,2,1,0:T(2,128)(2,1)S(1)} async-done(((bf16[256,5,2,128]{3,2,1,0:T(2,128)(2,1)}), bf16[256,5,2,128]{3,2,1,0:T(2,128)(2,1)S(1)}, u32[]{:S(2)}, u32[]{:S(2)}) %all-to-all-start) | async-done | bytes 655392 | tf_op jit(solution)/shard_map/to_channels/all_to_all | solution.py:260
  41.1 0.1 slice.3
  41.2 4.0 %collective-permute-start = (bf16[512,128]{1,0:T(8,128)(2,1)S(1)}, bf16[512,128]{1,0:T(8,128)(2,1)S(1)}, u32[]{:S(2)}, u32[]{:S(2)}) collective-permute-start(bf16[512,128]{1,0:T(8,128)(2,1)S(1)} %bitcast.13), channel_id=1, source_target_pairs={{0,1},{1,0},{2,3},{3,2},{4,5},{5,4},{6,7},{7,6},{8,9},{9,8},{10,11... | collective-permute-start | bytes 393224 | tf_op jit(solution)/shard_map/signal_swap/ppermute | solution.py:288
  45.2 0.7 own_positions.1
  46.0 0.2 collective-permute-done.other_ref
  46.2 0.0 copy-done.1
  46.2 0.0 copy-start.6
  46.2 3.4 %spectrum.1 = (f32[256,256]{1,0:T(8,128)S(1)}, f32[256,256]{1,0:T(8,128)S(1)}) custom-call(bf16[2,2,256,1024]{3,2,1,0:T(8,128)(2,1)S(1)} %copy-done.1, bf16[512,128]{1,0:T(8,128)(2,1)S(1)} %collective-permute-done.other_ref, bf16[2,1024,256]{2,1,0:T(8,128)(2,1)S(1)} %get-tuple-element.34.forward_ref, f32[1024,256]{1,0:T(8,128)S(1)} %get-tuple-element.37.field_ref, ...), custom_call_target="tpu_custom_call" | custom-call | tf_op jit(solution)/shard_map/spectrum/pallas_call | solution.py:297
  49.7 2.3 %collective-permute-start.1 = (f32[256,256]{1,0:T(8,128)S(1)}, f32[256,256]{1,0:T(8,128)S(1)}, u32[]{:S(2)}, u32[]{:S(2)}) collective-permute-start(f32[256,256]{1,0:T(8,128)S(1)} %get-tuple-element.42), channel_id=1, source_target_pairs={{0,1},{1,0},{2,3},{3,2},{4,5},{5,4},{6,7},{7,6},{8,9},{9,8},{10,11... | collective-permute-start | bytes 786440 | tf_op jit(solution)/shard_map/result_swap/ppermute | solution.py:303
  51.9 1.1 %collective-permute-done.1.came_ref = f32[256,256]{1,0:T(8,128)S(1)} collective-permute-done((f32[256,256]{1,0:T(8,128)S(1)}, f32[256,256]{1,0:T(8,128)S(1)}, u32[]{:S(2)}, u32[]{:S(2)}) %collective-permute-start.1) | collective-permute-done | bytes 262176 | tf_op jit(solution)/shard_map/result_swap/ppermute | solution.py:303
  53.1 0.7 add_cores.1
  53.8 16.6 %all-to-all-start.1 = ((bf16[256,1,2,128]{3,2,1,0:T(2,128)(2,1)}), bf16[256,1,2,128]{3,2,1,0:T(2,128)(2,1)S(1)}, u32[]{:S(2)}, u32[]{:S(2)}) async-start(bf16[256,1,2,128]{3,2,1,0:T(2,128)(2,1)} %bitcast.5), calls=%async_computation.1 | async-start | bytes 262144 | tf_op jit(solution)/shard_map/to_positions/all_to_all | solution.py:260
  70.4 0.0 copy-done.8
  70.4 0.1 copy.17.gain_ref
  70.6 3.5 %all-to-all-done.1 = bf16[256,1,2,128]{3,2,1,0:T(2,128)(2,1)S(1)} async-done(((bf16[256,1,2,128]{3,2,1,0:T(2,128)(2,1)}), bf16[256,1,2,128]{3,2,1,0:T(2,128)(2,1)S(1)}, u32[]{:S(2)}, u32[]{:S(2)}) %all-to-all-start.1) | async-done | bytes 131104 | tf_op jit(solution)/shard_map/to_positions/all_to_all | solution.py:260
  74.1 0.8 %gate.1 = f32[256,256]{1,0:T(8,128)} custom-call(bf16[512,128]{1,0:T(8,128)(2,1)S(1)} %bitcast.10, bf16[256,256]{1,0:T(8,128)(2,1)S(1)} %copy-done.6, bf16[256,256]{1,0:T(8,128)(2,1)S(1)} %copy-done.3, bf16[256,256]{1,0:T(8,128)(2,1)S(1)} %copy-done.4, f32[256,1]{1,0:T(8,128)S(1)} %copy.17.gain_ref), custom_call_target="tpu_custom_call" | custom-call | tf_op jit(solution)/shard_map/gate/pallas_call | solution.py:312
  (10 shorter events, 0.0 us)
Async XLA Ops:
  0.0 27.0 %copy-start.5 = (f32[2,2,32,384]{3,2,1,0:T(8,128)S(1)}, f32[2,2,32,384]{3,2,1,0:T(8,128)}, u32[]{:S(2)}) copy-start(f32[2,2,32,384]{3,2,1,0:T(8,128)} %constant.11.clone.refs_1_) | copy-start | bytes 589828
  0.0 27.0 %copy-start.7 = (f32[2,2,16,384]{3,2,1,0:T(8,128)S(1)}, f32[2,2,16,384]{3,2,1,0:T(8,128)}, u32[]{:S(2)}) copy-start(f32[2,2,16,384]{3,2,1,0:T(8,128)} %constant.12.clone.refs_2_) | copy-start | bytes 294916
  2.2 39.0 %all-to-all-start = ((bf16[256,5,2,128]{3,2,1,0:T(2,128)(2,1)}), bf16[256,5,2,128]{3,2,1,0:T(2,128)(2,1)S(1)}, u32[]{:S(2)}, u32[]{:S(2)}) async-start(bf16[256,5,2,128]{3,2,1,0:T(2,128)(2,1)} %bitcast.11), calls=%async_computation | async-start | bytes 1310720 | tf_op jit(solution)/shard_map/to_channels/all_to_all | solution.py:260
  27.0 1.6 %copy-start = (bf16[2,2,1024,256]{3,2,1,0:T(8,128)(2,1)S(1)}, bf16[2,2,1024,256]{3,2,1,0:T(8,128)(2,1)}, u32[]{:S(2)}) copy-start(bf16[2,2,1024,256]{3,2,1,0:T(8,128)(2,1)} %constant.10.clone.refs_0_) | copy-start | bytes 6291460
  28.6 1.2 %copy-start.2 = (bf16[2,512,512]{2,1,0:T(8,128)(2,1)S(1)}, bf16[2,512,512]{2,1,0:T(8,128)(2,1)}, u32[]{:S(2)}) copy-start(bf16[2,512,512]{2,1,0:T(8,128)(2,1)} %constant.13.clone.refs_3_) | copy-start | bytes 3145732
  41.1 5.1 %copy-start.1 = (bf16[2,2,256,1024]{3,2,1,0:T(8,128)(2,1)S(1)}, bf16[2,2,256,1024]{3,2,1,0:T(8,128)(2,1)}, u32[]{:S(2)}) copy-start(bf16[2,2,256,1024]{3,2,1,0:T(8,128)(2,1)} %constant.14.clone.backward_hbm) | copy-start | bytes 6291460
  41.2 5.0 %collective-permute-start = (bf16[512,128]{1,0:T(8,128)(2,1)S(1)}, bf16[512,128]{1,0:T(8,128)(2,1)S(1)}, u32[]{:S(2)}, u32[]{:S(2)}) collective-permute-start(bf16[512,128]{1,0:T(8,128)(2,1)S(1)} %bitcast.13), channel_id=1, source_target_pairs={{0,1},{1,0},{2,3},{3,2},{4,5},{5,4},{6,7},{7,6},{8,9},{9,8},{10,11... | collective-permute-start | bytes 393224 | tf_op jit(solution)/shard_map/signal_swap/ppermute | solution.py:288
  46.2 24.2 %copy-start.8 = (f32[256]{0:T(256)S(1)}, f32[256]{0:T(256)}, u32[]{:S(2)}) copy-start(f32[256]{0:T(256)} %param.14) | copy-start | bytes 3076
  46.2 27.8 %copy-start.3 = (bf16[256,256]{1,0:T(8,128)(2,1)S(1)}, bf16[256,256]{1,0:T(8,128)(2,1)}, u32[]{:S(2)}) copy-start(bf16[256,256]{1,0:T(8,128)(2,1)} %k_ref.1) | copy-start | bytes 393220
  46.2 27.8 %copy-start.4 = (bf16[256,256]{1,0:T(8,128)(2,1)S(1)}, bf16[256,256]{1,0:T(8,128)(2,1)}, u32[]{:S(2)}) copy-start(bf16[256,256]{1,0:T(8,128)(2,1)} %v_ref.1) | copy-start | bytes 393220
  46.2 27.8 %copy-start.6 = (bf16[256,256]{1,0:T(8,128)(2,1)S(1)}, bf16[256,256]{1,0:T(8,128)(2,1)}, u32[]{:S(2)}) copy-start(bf16[256,256]{1,0:T(8,128)(2,1)} %q_ref.1) | copy-start | bytes 393220
  49.7 3.4 %collective-permute-start.1 = (f32[256,256]{1,0:T(8,128)S(1)}, f32[256,256]{1,0:T(8,128)S(1)}, u32[]{:S(2)}, u32[]{:S(2)}) collective-permute-start(f32[256,256]{1,0:T(8,128)S(1)} %get-tuple-element.42), channel_id=1, source_target_pairs={{0,1},{1,0},{2,3},{3,2},{4,5},{5,4},{6,7},{7,6},{8,9},{9,8},{10,11... | collective-permute-start | bytes 786440 | tf_op jit(solution)/shard_map/result_swap/ppermute | solution.py:303
  53.8 20.3 %all-to-all-start.1 = ((bf16[256,1,2,128]{3,2,1,0:T(2,128)(2,1)}), bf16[256,1,2,128]{3,2,1,0:T(2,128)(2,1)S(1)}, u32[]{:S(2)}, u32[]{:S(2)}) async-start(bf16[256,1,2,128]{3,2,1,0:T(2,128)(2,1)} %bitcast.5), calls=%async_computation.1 | async-start | bytes 262144 | tf_op jit(solution)/shard_map/to_positions/all_to_all | solution.py:260

commit v5 on v4

--- a/solution.py
+++ b/solution.py
@@ -220,14 +220,24 @@
     out_ref[...] = wide[: out_ref.shape[0], :].astype(jnp.bfloat16)
 
 
-def gate_kernel(got_ref, q_ref, k_ref, v_ref, gain_ref, out_ref, wide):
-    channels = q_ref.shape[0]
-    wide[: got_ref.shape[0], :] = got_ref[...].astype(jnp.float32)
-    conv = joined(wide, 0, 2, channels)
-    signal = (k_ref[...].astype(jnp.float32) * v_ref[...].astype(jnp.float32)).astype(jnp.bfloat16)
-    out_ref[...] = q_ref[...].astype(jnp.float32) * (
-        conv + gain_ref[...] * signal.astype(jnp.float32)
-    )
+def gate_kernel(got_ref, q_ref, k_ref, v_ref, gain_ref, out_hbm, wide, out_ref, sems):
+    chunk = q_ref.shape[0] // CHUNKS
+    send = []
+    for index in range(CHUNKS):
+        rows = slice(index * chunk, (index + 1) * chunk)
+        both = slice(2 * index * chunk, 2 * (index + 1) * chunk)
+        wide[both, :] = got_ref[both, :].astype(jnp.float32)
+        conv = joined(wide, 2 * index * chunk, 2, chunk)
+        signal = k_ref[rows, :].astype(jnp.float32) * v_ref[rows, :].astype(jnp.float32)
+        signal = signal.astype(jnp.bfloat16).astype(jnp.float32)
+        out_ref[rows, :] = q_ref[rows, :].astype(jnp.float32) * (conv + gain_ref[rows, :] * signal)
+        part = pl.ds(index * chunk, chunk)
+        send.append(
+            pltpu.make_async_copy(out_ref.at[part], out_hbm.at[part], sems.at[index])
+        )
+        send[index].start()
+    for copy in send:
+        copy.wait()
 
 
 def call(kernel, shapes, scratch, megabytes, anywhere=0, out_anywhere=False, operands=0):
@@ -311,7 +321,8 @@
     with jax.named_scope("gate"):
         return call(
             gate_kernel, shape((channels, length), f32),
-            [pltpu.VMEM((2 * channels + SPARE, LANES), f32)], 4,
+            [pltpu.VMEM((2 * channels + SPARE, LANES), f32), pltpu.VMEM((channels, length), f32),
+             pltpu.SemaphoreType.DMA((CHUNKS,))], 4, out_anywhere=True,
         )(returned.reshape(2 * channels, LANES), q_proj, k_proj, v_proj, skip_gain[:, None])
 
 

time: 75.4 us -> 75.4 us (level)
  no operation moved by 1% of the time
where the time goes in v5:
time: 75.4 us; the launch traced here: 74.9 us
  starting transfers between devices  47.7 us (63%)
  waiting for transfers between devices  15.8 us (21%)
  Pallas kernels  8.16 us (11%)
  local copies, waits for them, and re-layouts  3.06 us (4%)
    all_to_all x2, starting transfers between devices, exchange(): lax.all_to_all(tensor.reshape(pairs, pieces, 2, LANES), both_axes, 0, 0,...  41.4 us
    all_to_all x2, waiting for transfers between devices, exchange(): lax.all_to_all(tensor.reshape(pairs, pieces, 2, LANES), both_axes, 0, 0,...  14.4 us
    ppermute x1, starting transfers between devices, body(): other = lax.ppermute(incoming[:, 4].reshape(2 * pairs, LANES), 'row', swap)  3.99 us
    pallas_call x1, Pallas kernels, body(): call(spectrum_kernel, [shape((pairs, length), f32)] * 2, [pltpu.VMEM((2 *...  3.42 us
    unnamed x18, local copies, waits for them, and re-layouts  2.84 us
    ppermute x1, starting transfers between devices, body(): came = lax.ppermute(sent, 'row', swap)  2.28 us
    pallas_call x1, Pallas kernels, body(): call(pack_kernel, shape((10 * channels, LANES), bf16), [pltpu.VMEM((chann...  2.15 us
  transfers between devices with their start and end apart: 4, of which 4 were waited for; matrix products, arithmetic and copies ran while one was open for 0% of the time, Pallas kernels for 1%

profile of v5, /device:TPU:1, one launch (start us, length us, event | category | flops | bytes accessed | tf_op | source)
XLA Modules:
  0.0 74.9 jit_solution(4569133587118813731)
XLA Ops:
  0.0 2.1 %pack.1 = bf16[2560,128]{1,0:T(8,128)(2,1)} custom-call(bf16[256,256]{1,0:T(8,128)(2,1)} %k_ref.1, bf16[256,256]{1,0:T(8,128)(2,1)} %v_ref.1, f32[4,512,128]{2,1,0:T(8,128)} %bitcast.12), custom_call_target="tpu_custom_call" | custom-call | tf_op jit(solution)/shard_map/pack/pallas_call | solution.py:276
  2.2 24.8 %all-to-all-start = ((bf16[256,5,2,128]{3,2,1,0:T(2,128)(2,1)}), bf16[256,5,2,128]{3,2,1,0:T(2,128)(2,1)S(1)}, u32[]{:S(2)}, u32[]{:S(2)}) async-start(bf16[256,5,2,128]{3,2,1,0:T(2,128)(2,1)} %bitcast.11), calls=%async_computation | async-start | bytes 1310720 | tf_op jit(solution)/shard_map/to_channels/all_to_all | solution.py:270
  27.0 0.0 copy-done.5
  27.0 0.0 copy-done.7
  27.0 0.0 copy-start
  27.0 1.6 %copy-done = bf16[2,2,1024,256]{3,2,1,0:T(8,128)(2,1)S(1)} copy-done((bf16[2,2,1024,256]{3,2,1,0:T(8,128)(2,1)S(1)}, bf16[2,2,1024,256]{3,2,1,0:T(8,128)(2,1)}, u32[]{:S(2)}) %copy-start) | copy-done | bytes 2097176
  28.6 1.2 %copy-done.2 = bf16[2,512,512]{2,1,0:T(8,128)(2,1)S(1)} copy-done((bf16[2,512,512]{2,1,0:T(8,128)(2,1)S(1)}, bf16[2,512,512]{2,1,0:T(8,128)(2,1)}, u32[]{:S(2)}) %copy-start.2) | copy-done | bytes 1048600
  29.8 0.4 tables.1
  30.2 11.0 %all-to-all-done = bf16[256,5,2,128]{3,2,1,0:T(2,128)(2,1)S(1)} async-done(((bf16[256,5,2,128]{3,2,1,0:T(2,128)(2,1)}), bf16[256,5,2,128]{3,2,1,0:T(2,128)(2,1)S(1)}, u32[]{:S(2)}, u32[]{:S(2)}) %all-to-all-start) | async-done | bytes 655392 | tf_op jit(solution)/shard_map/to_channels/all_to_all | solution.py:270
  41.1 0.1 slice.3
  41.2 4.0 %collective-permute-start = (bf16[512,128]{1,0:T(8,128)(2,1)S(1)}, bf16[512,128]{1,0:T(8,128)(2,1)S(1)}, u32[]{:S(2)}, u32[]{:S(2)}) collective-permute-start(bf16[512,128]{1,0:T(8,128)(2,1)S(1)} %bitcast.13), channel_id=1, source_target_pairs={{0,1},{1,0},{2,3},{3,2},{4,5},{5,4},{6,7},{7,6},{8,9},{9,8},{10,11... | collective-permute-start | bytes 393224 | tf_op jit(solution)/shard_map/signal_swap/ppermute | solution.py:298
  45.2 0.7 own_positions.1
  46.0 0.2 collective-permute-done.other_ref
  46.2 0.0 copy-done.1
  46.2 0.0 copy-start.6
  46.2 3.4 %spectrum.1 = (f32[256,256]{1,0:T(8,128)S(1)}, f32[256,256]{1,0:T(8,128)S(1)}) custom-call(bf16[2,2,256,1024]{3,2,1,0:T(8,128)(2,1)S(1)} %copy-done.1, bf16[512,128]{1,0:T(8,128)(2,1)S(1)} %collective-permute-done.other_ref, bf16[2,1024,256]{2,1,0:T(8,128)(2,1)S(1)} %get-tuple-element.34.forward_ref, f32[1024,256]{1,0:T(8,128)S(1)} %get-tuple-element.37.field_ref, ...), custom_call_target="tpu_custom_call" | custom-call | tf_op jit(solution)/shard_map/spectrum/pallas_call | solution.py:307
  49.7 2.3 %collective-permute-start.1 = (f32[256,256]{1,0:T(8,128)S(1)}, f32[256,256]{1,0:T(8,128)S(1)}, u32[]{:S(2)}, u32[]{:S(2)}) collective-permute-start(f32[256,256]{1,0:T(8,128)S(1)} %get-tuple-element.42), channel_id=1, source_target_pairs={{0,1},{1,0},{2,3},{3,2},{4,5},{5,4},{6,7},{7,6},{8,9},{9,8},{10,11... | collective-permute-start | bytes 786440 | tf_op jit(solution)/shard_map/result_swap/ppermute | solution.py:313
  51.9 1.1 %collective-permute-done.1.came_ref = f32[256,256]{1,0:T(8,128)S(1)} collective-permute-done((f32[256,256]{1,0:T(8,128)S(1)}, f32[256,256]{1,0:T(8,128)S(1)}, u32[]{:S(2)}, u32[]{:S(2)}) %collective-permute-start.1) | collective-permute-done | bytes 262176 | tf_op jit(solution)/shard_map/result_swap/ppermute | solution.py:313
  53.1 0.7 add_cores.1
  53.8 16.6 %all-to-all-start.1 = ((bf16[256,1,2,128]{3,2,1,0:T(2,128)(2,1)}), bf16[256,1,2,128]{3,2,1,0:T(2,128)(2,1)S(1)}, u32[]{:S(2)}, u32[]{:S(2)}) async-start(bf16[256,1,2,128]{3,2,1,0:T(2,128)(2,1)} %bitcast.5), calls=%async_computation.1 | async-start | bytes 262144 | tf_op jit(solution)/shard_map/to_positions/all_to_all | solution.py:270
  70.4 0.1 copy.17.gain_ref
  70.6 3.5 %all-to-all-done.1 = bf16[256,1,2,128]{3,2,1,0:T(2,128)(2,1)S(1)} async-done(((bf16[256,1,2,128]{3,2,1,0:T(2,128)(2,1)}), bf16[256,1,2,128]{3,2,1,0:T(2,128)(2,1)S(1)}, u32[]{:S(2)}, u32[]{:S(2)}) %all-to-all-start.1) | async-done | bytes 131104 | tf_op jit(solution)/shard_map/to_positions/all_to_all | solution.py:270
  74.0 0.0 copy-done.3
  74.1 0.8 %gate.1 = f32[256,256]{1,0:T(8,128)} custom-call(bf16[512,128]{1,0:T(8,128)(2,1)S(1)} %bitcast.10, bf16[256,256]{1,0:T(8,128)(2,1)S(1)} %copy-done.6, bf16[256,256]{1,0:T(8,128)(2,1)S(1)} %copy-done.3, bf16[256,256]{1,0:T(8,128)(2,1)S(1)} %copy-done.4, f32[256,1]{1,0:T(8,128)S(1)} %copy.17.gain_ref), custom_call_target="tpu_custom_call" | custom-call | tf_op jit(solution)/shard_map/gate/pallas_call | solution.py:322
  (10 shorter events, 0.0 us)
Async XLA Ops:
  0.0 27.0 %copy-start.5 = (f32[2,2,32,384]{3,2,1,0:T(8,128)S(1)}, f32[2,2,32,384]{3,2,1,0:T(8,128)}, u32[]{:S(2)}) copy-start(f32[2,2,32,384]{3,2,1,0:T(8,128)} %constant.11.clone.refs_1_) | copy-start | bytes 589828
  0.0 27.0 %copy-start.7 = (f32[2,2,16,384]{3,2,1,0:T(8,128)S(1)}, f32[2,2,16,384]{3,2,1,0:T(8,128)}, u32[]{:S(2)}) copy-start(f32[2,2,16,384]{3,2,1,0:T(8,128)} %constant.12.clone.refs_2_) | copy-start | bytes 294916
  2.2 39.0 %all-to-all-start = ((bf16[256,5,2,128]{3,2,1,0:T(2,128)(2,1)}), bf16[256,5,2,128]{3,2,1,0:T(2,128)(2,1)S(1)}, u32[]{:S(2)}, u32[]{:S(2)}) async-start(bf16[256,5,2,128]{3,2,1,0:T(2,128)(2,1)} %bitcast.11), calls=%async_computation | async-start | bytes 1310720 | tf_op jit(solution)/shard_map/to_channels/all_to_all | solution.py:270
  27.0 1.6 %copy-start = (bf16[2,2,1024,256]{3,2,1,0:T(8,128)(2,1)S(1)}, bf16[2,2,1024,256]{3,2,1,0:T(8,128)(2,1)}, u32[]{:S(2)}) copy-start(bf16[2,2,1024,256]{3,2,1,0:T(8,128)(2,1)} %constant.10.clone.refs_0_) | copy-start | bytes 6291460
  28.6 1.2 %copy-start.2 = (bf16[2,512,512]{2,1,0:T(8,128)(2,1)S(1)}, bf16[2,512,512]{2,1,0:T(8,128)(2,1)}, u32[]{:S(2)}) copy-start(bf16[2,512,512]{2,1,0:T(8,128)(2,1)} %constant.13.clone.refs_3_) | copy-start | bytes 3145732
  41.1 5.1 %copy-start.1 = (bf16[2,2,256,1024]{3,2,1,0:T(8,128)(2,1)S(1)}, bf16[2,2,256,1024]{3,2,1,0:T(8,128)(2,1)}, u32[]{:S(2)}) copy-start(bf16[2,2,256,1024]{3,2,1,0:T(8,128)(2,1)} %constant.14.clone.backward_hbm) | copy-start | bytes 6291460
  41.2 5.0 %collective-permute-start = (bf16[512,128]{1,0:T(8,128)(2,1)S(1)}, bf16[512,128]{1,0:T(8,128)(2,1)S(1)}, u32[]{:S(2)}, u32[]{:S(2)}) collective-permute-start(bf16[512,128]{1,0:T(8,128)(2,1)S(1)} %bitcast.13), channel_id=1, source_target_pairs={{0,1},{1,0},{2,3},{3,2},{4,5},{5,4},{6,7},{7,6},{8,9},{9,8},{10,11... | collective-permute-start | bytes 393224 | tf_op jit(solution)/shard_map/signal_swap/ppermute | solution.py:298
  46.2 24.2 %copy-start.8 = (f32[256]{0:T(256)S(1)}, f32[256]{0:T(256)}, u32[]{:S(2)}) copy-start(f32[256]{0:T(256)} %param.14) | copy-start | bytes 3076
  46.2 27.8 %copy-start.3 = (bf16[256,256]{1,0:T(8,128)(2,1)S(1)}, bf16[256,256]{1,0:T(8,128)(2,1)}, u32[]{:S(2)}) copy-start(bf16[256,256]{1,0:T(8,128)(2,1)} %k_ref.1) | copy-start | bytes 393220
  46.2 27.8 %copy-start.4 = (bf16[256,256]{1,0:T(8,128)(2,1)S(1)}, bf16[256,256]{1,0:T(8,128)(2,1)}, u32[]{:S(2)}) copy-start(bf16[256,256]{1,0:T(8,128)(2,1)} %v_ref.1) | copy-start | bytes 393220
  46.2 27.8 %copy-start.6 = (bf16[256,256]{1,0:T(8,128)(2,1)S(1)}, bf16[256,256]{1,0:T(8,128)(2,1)}, u32[]{:S(2)}) copy-start(bf16[256,256]{1,0:T(8,128)(2,1)} %q_ref.1) | copy-start | bytes 393220
  49.7 3.4 %collective-permute-start.1 = (f32[256,256]{1,0:T(8,128)S(1)}, f32[256,256]{1,0:T(8,128)S(1)}, u32[]{:S(2)}, u32[]{:S(2)}) collective-permute-start(f32[256,256]{1,0:T(8,128)S(1)} %get-tuple-element.42), channel_id=1, source_target_pairs={{0,1},{1,0},{2,3},{3,2},{4,5},{5,4},{6,7},{7,6},{8,9},{9,8},{10,11... | collective-permute-start | bytes 786440 | tf_op jit(solution)/shard_map/result_swap/ppermute | solution.py:313
  53.8 20.3 %all-to-all-start.1 = ((bf16[256,1,2,128]{3,2,1,0:T(2,128)(2,1)}), bf16[256,1,2,128]{3,2,1,0:T(2,128)(2,1)S(1)}, u32[]{:S(2)}, u32[]{:S(2)}) async-start(bf16[256,1,2,128]{3,2,1,0:T(2,128)(2,1)} %bitcast.5), calls=%async_computation.1 | async-start | bytes 262144 | tf_op jit(solution)/shard_map/to_positions/all_to_all | solution.py:270

commit v6 on v5

--- a/solution.py
+++ b/solution.py
@@ -111,16 +111,16 @@
         copy.start()
     fetch[0].wait()
     fetch[1].wait()
-    product = k_ref[...].astype(jnp.float32) * v_ref[...].astype(jnp.float32)
-    product = product.astype(jnp.bfloat16).astype(jnp.float32)
-    for half in range(2):
-        wide[pl.ds(8 + half, channels, stride=10), :] = product[
-            :, half * LANES : (half + 1) * LANES
-        ]
     send = []
     for index in range(CHUNKS):
         fetch[2 + index].wait()
         first = 10 * index * chunk
+        mine = slice(index * chunk, (index + 1) * chunk)
+        product = k_ref[mine, :].astype(jnp.float32) * v_ref[mine, :].astype(jnp.float32)
+        for half in range(2):
+            wide[pl.ds(first + 8 + half, chunk, stride=10), :] = product[
+                :, half * LANES : (half + 1) * LANES
+            ]
         for part in range(2):
             for low in range(2):
                 for half in range(2):

time: 75.4 us -> 75.4 us (level)
  no operation moved by 1% of the time
where the time goes in v6:
time: 75.4 us; the launch traced here: 74.9 us
  starting transfers between devices  47.7 us (63%)
  waiting for transfers between devices  15.8 us (21%)
  Pallas kernels  8.16 us (11%)
  local copies, waits for them, and re-layouts  3.06 us (4%)
    all_to_all x2, starting transfers between devices, exchange(): lax.all_to_all(tensor.reshape(pairs, pieces, 2, LANES), both_axes, 0, 0,...  41.4 us
    all_to_all x2, waiting for transfers between devices, exchange(): lax.all_to_all(tensor.reshape(pairs, pieces, 2, LANES), both_axes, 0, 0,...  14.4 us
    ppermute x1, starting transfers between devices, body(): other = lax.ppermute(incoming[:, 4].reshape(2 * pairs, LANES), 'row', swap)  3.99 us
    pallas_call x1, Pallas kernels, body(): call(spectrum_kernel, [shape((pairs, length), f32)] * 2, [pltpu.VMEM((2 *...  3.42 us
    unnamed x18, local copies, waits for them, and re-layouts  2.84 us
    ppermute x1, starting transfers between devices, body(): came = lax.ppermute(sent, 'row', swap)  2.27 us
    pallas_call x1, Pallas kernels, body(): call(pack_kernel, shape((10 * channels, LANES), bf16), [pltpu.VMEM((chann...  2.16 us
  transfers between devices with their start and end apart: 4, of which 4 were waited for; matrix products, arithmetic and copies ran while one was open for 0% of the time, Pallas kernels for 1%

profile of v6, /device:TPU:1, one launch (start us, length us, event | category | flops | bytes accessed | tf_op | source)
XLA Modules:
  0.0 74.9 jit_solution(9709883810891606085)
XLA Ops:
  0.0 2.2 %pack.1 = bf16[2560,128]{1,0:T(8,128)(2,1)} custom-call(bf16[256,256]{1,0:T(8,128)(2,1)} %k_ref.1, bf16[256,256]{1,0:T(8,128)(2,1)} %v_ref.1, f32[4,512,128]{2,1,0:T(8,128)} %bitcast.12), custom_call_target="tpu_custom_call" | custom-call | tf_op jit(solution)/shard_map/pack/pallas_call | solution.py:276
  2.2 24.8 %all-to-all-start = ((bf16[256,5,2,128]{3,2,1,0:T(2,128)(2,1)}), bf16[256,5,2,128]{3,2,1,0:T(2,128)(2,1)S(1)}, u32[]{:S(2)}, u32[]{:S(2)}) async-start(bf16[256,5,2,128]{3,2,1,0:T(2,128)(2,1)} %bitcast.11), calls=%async_computation | async-start | bytes 1310720 | tf_op jit(solution)/shard_map/to_channels/all_to_all | solution.py:270
  27.0 0.0 copy-done.5
  27.0 0.0 copy-done.7
  27.0 0.0 copy-start
  27.0 1.6 %copy-done = bf16[2,2,1024,256]{3,2,1,0:T(8,128)(2,1)S(1)} copy-done((bf16[2,2,1024,256]{3,2,1,0:T(8,128)(2,1)S(1)}, bf16[2,2,1024,256]{3,2,1,0:T(8,128)(2,1)}, u32[]{:S(2)}) %copy-start) | copy-done | bytes 2097176
  28.6 1.2 %copy-done.2 = bf16[2,512,512]{2,1,0:T(8,128)(2,1)S(1)} copy-done((bf16[2,512,512]{2,1,0:T(8,128)(2,1)S(1)}, bf16[2,512,512]{2,1,0:T(8,128)(2,1)}, u32[]{:S(2)}) %copy-start.2) | copy-done | bytes 1048600
  29.8 0.4 tables.1
  30.2 11.0 %all-to-all-done = bf16[256,5,2,128]{3,2,1,0:T(2,128)(2,1)S(1)} async-done(((bf16[256,5,2,128]{3,2,1,0:T(2,128)(2,1)}), bf16[256,5,2,128]{3,2,1,0:T(2,128)(2,1)S(1)}, u32[]{:S(2)}, u32[]{:S(2)}) %all-to-all-start) | async-done | bytes 655392 | tf_op jit(solution)/shard_map/to_channels/all_to_all | solution.py:270
  41.1 0.1 slice.3
  41.2 4.0 %collective-permute-start = (bf16[512,128]{1,0:T(8,128)(2,1)S(1)}, bf16[512,128]{1,0:T(8,128)(2,1)S(1)}, u32[]{:S(2)}, u32[]{:S(2)}) collective-permute-start(bf16[512,128]{1,0:T(8,128)(2,1)S(1)} %bitcast.13), channel_id=1, source_target_pairs={{0,1},{1,0},{2,3},{3,2},{4,5},{5,4},{6,7},{7,6},{8,9},{9,8},{10,11... | collective-permute-start | bytes 393224 | tf_op jit(solution)/shard_map/signal_swap/ppermute | solution.py:298
  45.2 0.7 own_positions.1
  45.9 0.3 collective-permute-done.other_ref
  46.2 0.0 copy-done.1
  46.2 0.0 copy-start.6
  46.2 3.4 %spectrum.1 = (f32[256,256]{1,0:T(8,128)S(1)}, f32[256,256]{1,0:T(8,128)S(1)}) custom-call(bf16[2,2,256,1024]{3,2,1,0:T(8,128)(2,1)S(1)} %copy-done.1, bf16[512,128]{1,0:T(8,128)(2,1)S(1)} %collective-permute-done.other_ref, bf16[2,1024,256]{2,1,0:T(8,128)(2,1)S(1)} %get-tuple-element.34.forward_ref, f32[1024,256]{1,0:T(8,128)S(1)} %get-tuple-element.37.field_ref, ...), custom_call_target="tpu_custom_call" | custom-call | tf_op jit(solution)/shard_map/spectrum/pallas_call | solution.py:307
  49.7 2.3 %collective-permute-start.1 = (f32[256,256]{1,0:T(8,128)S(1)}, f32[256,256]{1,0:T(8,128)S(1)}, u32[]{:S(2)}, u32[]{:S(2)}) collective-permute-start(f32[256,256]{1,0:T(8,128)S(1)} %get-tuple-element.42), channel_id=1, source_target_pairs={{0,1},{1,0},{2,3},{3,2},{4,5},{5,4},{6,7},{7,6},{8,9},{9,8},{10,11... | collective-permute-start | bytes 786440 | tf_op jit(solution)/shard_map/result_swap/ppermute | solution.py:313
  51.9 1.1 %collective-permute-done.1.came_ref = f32[256,256]{1,0:T(8,128)S(1)} collective-permute-done((f32[256,256]{1,0:T(8,128)S(1)}, f32[256,256]{1,0:T(8,128)S(1)}, u32[]{:S(2)}, u32[]{:S(2)}) %collective-permute-start.1) | collective-permute-done | bytes 262176 | tf_op jit(solution)/shard_map/result_swap/ppermute | solution.py:313
  53.1 0.7 add_cores.1
  53.8 16.6 %all-to-all-start.1 = ((bf16[256,1,2,128]{3,2,1,0:T(2,128)(2,1)}), bf16[256,1,2,128]{3,2,1,0:T(2,128)(2,1)S(1)}, u32[]{:S(2)}, u32[]{:S(2)}) async-start(bf16[256,1,2,128]{3,2,1,0:T(2,128)(2,1)} %bitcast.5), calls=%async_computation.1 | async-start | bytes 262144 | tf_op jit(solution)/shard_map/to_positions/all_to_all | solution.py:270
  70.4 0.0 copy-done.8
  70.4 0.1 copy.17.gain_ref
  70.6 3.5 %all-to-all-done.1 = bf16[256,1,2,128]{3,2,1,0:T(2,128)(2,1)S(1)} async-done(((bf16[256,1,2,128]{3,2,1,0:T(2,128)(2,1)}), bf16[256,1,2,128]{3,2,1,0:T(2,128)(2,1)S(1)}, u32[]{:S(2)}, u32[]{:S(2)}) %all-to-all-start.1) | async-done | bytes 131104 | tf_op jit(solution)/shard_map/to_positions/all_to_all | solution.py:270
  74.1 0.8 %gate.1 = f32[256,256]{1,0:T(8,128)} custom-call(bf16[512,128]{1,0:T(8,128)(2,1)S(1)} %bitcast.10, bf16[256,256]{1,0:T(8,128)(2,1)S(1)} %copy-done.6, bf16[256,256]{1,0:T(8,128)(2,1)S(1)} %copy-done.3, bf16[256,256]{1,0:T(8,128)(2,1)S(1)} %copy-done.4, f32[256,1]{1,0:T(8,128)S(1)} %copy.17.gain_ref), custom_call_target="tpu_custom_call" | custom-call | tf_op jit(solution)/shard_map/gate/pallas_call | solution.py:322
  (10 shorter events, 0.0 us)
Async XLA Ops:
  0.0 27.0 %copy-start.5 = (f32[2,2,32,384]{3,2,1,0:T(8,128)S(1)}, f32[2,2,32,384]{3,2,1,0:T(8,128)}, u32[]{:S(2)}) copy-start(f32[2,2,32,384]{3,2,1,0:T(8,128)} %constant.11.clone.refs_1_) | copy-start | bytes 589828
  0.0 27.0 %copy-start.7 = (f32[2,2,16,384]{3,2,1,0:T(8,128)S(1)}, f32[2,2,16,384]{3,2,1,0:T(8,128)}, u32[]{:S(2)}) copy-start(f32[2,2,16,384]{3,2,1,0:T(8,128)} %constant.12.clone.refs_2_) | copy-start | bytes 294916
  2.2 39.0 %all-to-all-start = ((bf16[256,5,2,128]{3,2,1,0:T(2,128)(2,1)}), bf16[256,5,2,128]{3,2,1,0:T(2,128)(2,1)S(1)}, u32[]{:S(2)}, u32[]{:S(2)}) async-start(bf16[256,5,2,128]{3,2,1,0:T(2,128)(2,1)} %bitcast.11), calls=%async_computation | async-start | bytes 1310720 | tf_op jit(solution)/shard_map/to_channels/all_to_all | solution.py:270
  27.0 1.6 %copy-start = (bf16[2,2,1024,256]{3,2,1,0:T(8,128)(2,1)S(1)}, bf16[2,2,1024,256]{3,2,1,0:T(8,128)(2,1)}, u32[]{:S(2)}) copy-start(bf16[2,2,1024,256]{3,2,1,0:T(8,128)(2,1)} %constant.10.clone.refs_0_) | copy-start | bytes 6291460
  28.6 1.2 %copy-start.2 = (bf16[2,512,512]{2,1,0:T(8,128)(2,1)S(1)}, bf16[2,512,512]{2,1,0:T(8,128)(2,1)}, u32[]{:S(2)}) copy-start(bf16[2,512,512]{2,1,0:T(8,128)(2,1)} %constant.13.clone.refs_3_) | copy-start | bytes 3145732
  41.1 5.1 %copy-start.1 = (bf16[2,2,256,1024]{3,2,1,0:T(8,128)(2,1)S(1)}, bf16[2,2,256,1024]{3,2,1,0:T(8,128)(2,1)}, u32[]{:S(2)}) copy-start(bf16[2,2,256,1024]{3,2,1,0:T(8,128)(2,1)} %constant.14.clone.backward_hbm) | copy-start | bytes 6291460
  41.2 5.0 %collective-permute-start = (bf16[512,128]{1,0:T(8,128)(2,1)S(1)}, bf16[512,128]{1,0:T(8,128)(2,1)S(1)}, u32[]{:S(2)}, u32[]{:S(2)}) collective-permute-start(bf16[512,128]{1,0:T(8,128)(2,1)S(1)} %bitcast.13), channel_id=1, source_target_pairs={{0,1},{1,0},{2,3},{3,2},{4,5},{5,4},{6,7},{7,6},{8,9},{9,8},{10,11... | collective-permute-start | bytes 393224 | tf_op jit(solution)/shard_map/signal_swap/ppermute | solution.py:298
  46.2 24.2 %copy-start.8 = (f32[256]{0:T(256)S(1)}, f32[256]{0:T(256)}, u32[]{:S(2)}) copy-start(f32[256]{0:T(256)} %param.14) | copy-start | bytes 3076
  46.2 27.9 %copy-start.3 = (bf16[256,256]{1,0:T(8,128)(2,1)S(1)}, bf16[256,256]{1,0:T(8,128)(2,1)}, u32[]{:S(2)}) copy-start(bf16[256,256]{1,0:T(8,128)(2,1)} %k_ref.1) | copy-start | bytes 393220
  46.2 27.9 %copy-start.4 = (bf16[256,256]{1,0:T(8,128)(2,1)S(1)}, bf16[256,256]{1,0:T(8,128)(2,1)}, u32[]{:S(2)}) copy-start(bf16[256,256]{1,0:T(8,128)(2,1)} %v_ref.1) | copy-start | bytes 393220
  46.2 27.9 %copy-start.6 = (bf16[256,256]{1,0:T(8,128)(2,1)S(1)}, bf16[256,256]{1,0:T(8,128)(2,1)}, u32[]{:S(2)}) copy-start(bf16[256,256]{1,0:T(8,128)(2,1)} %q_ref.1) | copy-start | bytes 393220
  49.7 3.4 %collective-permute-start.1 = (f32[256,256]{1,0:T(8,128)S(1)}, f32[256,256]{1,0:T(8,128)S(1)}, u32[]{:S(2)}, u32[]{:S(2)}) collective-permute-start(f32[256,256]{1,0:T(8,128)S(1)} %get-tuple-element.42), channel_id=1, source_target_pairs={{0,1},{1,0},{2,3},{3,2},{4,5},{5,4},{6,7},{7,6},{8,9},{9,8},{10,11... | collective-permute-start | bytes 786440 | tf_op jit(solution)/shard_map/result_swap/ppermute | solution.py:313
  53.8 20.3 %all-to-all-start.1 = ((bf16[256,1,2,128]{3,2,1,0:T(2,128)(2,1)}), bf16[256,1,2,128]{3,2,1,0:T(2,128)(2,1)S(1)}, u32[]{:S(2)}, u32[]{:S(2)}) async-start(bf16[256,1,2,128]{3,2,1,0:T(2,128)(2,1)} %bitcast.5), calls=%async_computation.1 | async-start | bytes 262144 | tf_op jit(solution)/shard_map/to_positions/all_to_all | solution.py:270
